TPU v7x, 32 devices: a whole 2x2x4 slice. The times are simulated.
32 devices in a mesh: dev: 32 (over z, y, x, core).
Axes of the slice: x: 2, y: 2, z: 4, core: 2. Of those that a mesh axis runs over, the one named last changes fastest.
Arguments:
- tokens: bfloat16 [8192, 192], P('dev'), may hold values from -6 to 6
- ranges: int32 [32, 2], replicated, may hold values from 0 to 7936, as said below
- attn_in: bfloat16 [2, 110592], P(None, 'dev'), may hold values from -0.4375 to 0.4375
- attn_out: bfloat16 [2, 36864], P(None, 'dev'), may hold values from -3.5 to 3.5
- mlp_in: bfloat16 [2, 147456], P(None, 'dev'), may hold values from -0.4375 to 0.4375
- mlp_out: bfloat16 [2, 147456], P(None, 'dev'), may hold values from -0.21875 to 0.21875
- vectors: bfloat16 [2, 2304], P(None, 'dev'), may hold values from -0.75 to 1.5, as said below
- cotangent: bfloat16 [8192, 192], P('dev'), may hold values from -6 to 6
Outputs:
- activations: bfloat16 [8192, 192], P('dev')
- input_grad: float32 [8192, 192], P('dev')
- attn_in_grad: float32 [2, 110592], P(None, 'dev')
- attn_out_grad: float32 [2, 36864], P(None, 'dev')
- mlp_in_grad: float32 [2, 147456], P(None, 'dev')
- mlp_out_grad: float32 [2, 147456], P(None, 'dev')
- vectors_grad: float32 [2, 2304], P(None, 'dev')
Inputs may be any that keep to these rules, and one draw needn't show every extreme that they name: Row j gives the range of stream positions on device j; ranges follow one another from 0 to 7936; each device holds 240 to 256 tokens, some device exactly 256. `vectors`: norm gains lie within 0.5 to 1.5.
All inputs are finite; a program needn't handle non-finite values.
Results may differ from a plain program's by a relative error of at most 0.01.
Values may be sent and summed in bfloat16 or wider, within the bound.
A program may use at most 64 MiB of HBM per device.

v0:
```python
import functools
import math

import jax
import jax.numpy as jnp
from jax import lax
from jax.experimental import pallas as pl
from jax.experimental.pallas import tpu as pltpu
from jax.sharding import PartitionSpec as P

HD = 64
IMG_LEN = 197
ROWS = 208
IMAGES_HERE = 2
BLOCK = 16
MESH_ID = pl.DeviceIdType.MESH
bf16, f32 = jnp.bfloat16, jnp.float32
eps_norm = 1e-06
masked_fill = -1e30
vmem_bytes = 56 * 2**20


PIECES = 6


def bit_orders(n):
    down = list(range(n.bit_length() - 1))[::-1]
    lead, (p, q, r, s) = down[:-4], down[-4:]
    first, second = lead + [p, q, r, s], lead + [p, r, q, s]
    third, fourth = lead + [q, r, p, s], lead + [r, q, p, s]
    return first, second, third, first, second, fourth


def slot_of(dev, order, div=lax.div, rem=lax.rem):
    return sum(rem(div(dev, 2**b), 2) * 2**k for k, b in enumerate(order))


def greet(n, me, bits):
    barrier = pltpu.get_barrier_semaphore()
    others = [me + (1 - 2 * lax.rem(lax.div(me, 2**b), 2)) * 2**b for b in range(bits)]
    others += [lax.rem(me + 1, n), lax.rem(me + n - 1, n)]
    for other in others:
        pl.semaphore_signal(barrier, inc=1, device_id=(other,), device_id_type=MESH_ID)
    pl.semaphore_wait(barrier, len(others))
    return others


def remote(src, dst, send, recv, dev):
    return pltpu.make_async_remote_copy(
        src_ref=src, dst_ref=dst, send_sem=send, recv_sem=recv,
        device_id=(dev,), device_id_type=MESH_ID,
    )


def gather_kernel(n, blk, tok, cot, *refs):
    outs, (tok_out, cot_out, send, recv, hsend, hrecv) = refs[:PIECES], refs[PIECES:]
    me = lax.axis_index("dev")
    orders = bit_orders(n)
    bits = len(orders[0])
    slots = [slot_of(me, order) for order in orders]
    width = outs[0].shape[1]
    for c in range(PIECES):
        outs[c][pl.ds(slots[c] * BLOCK, BLOCK), :] = blk[:, c * width:(c + 1) * width]
    others = greet(n, me, bits)
    sent = []
    for k in range(bits):
        copies = []
        for c in range(PIECES):
            if k:
                sent[-PIECES].wait_recv()
            size = BLOCK * 2**k
            at = pl.ds(pl.multiple_of(lax.div(slots[c], 2**k) * size, BLOCK), size)
            copy = remote(
                outs[c].at[at, :], outs[c].at[at, :],
                send.at[c, k], recv.at[c, k], others[orders[c][k]],
            )
            copy.start()
            sent.append(copy)
        if k == 0:
            halo = [
                remote(tok, tok_out, hsend.at[0], hrecv.at[0], others[-1]),
                remote(cot, cot_out, hsend.at[1], hrecv.at[1], others[-1]),
            ]
            for copy in halo:
                copy.start()
    for copy in sent[-PIECES:]:
        copy.wait_recv()
    for copy in sent:
        copy.wait_send()
    for copy in halo:
        copy.wait()


def gather(n, blk, tok, cot):
    bits = n.bit_length() - 1
    width = blk.shape[1] // PIECES
    vm = pl.BlockSpec(memory_space=pltpu.VMEM)
    return pl.pallas_call(
        functools.partial(gather_kernel, n),
        out_shape=(jax.ShapeDtypeStruct((n * BLOCK, width), bf16),) * PIECES
        + (jax.ShapeDtypeStruct(tok.shape, bf16),) * 2,
        in_specs=[vm] + [pl.BlockSpec(memory_space=pl.ANY)] * 2,
        out_specs=(vm,) * (PIECES + 2),
        scratch_shapes=[
            pltpu.SemaphoreType.DMA((PIECES, bits)),
            pltpu.SemaphoreType.DMA((PIECES, bits)),
            pltpu.SemaphoreType.DMA((2,)),
            pltpu.SemaphoreType.DMA((2,)),
        ],
        compiler_params=pltpu.CompilerParams(
            collective_id=0, has_side_effects=True, vmem_limit_bytes=vmem_bytes
        ),
        name="gather_params",
    )(blk, tok, cot)


def scatter_kernel(n, *refs):
    sources, refs = refs[:PIECES], refs[PIECES:]
    act, act_up, dx, dx_up, result, act_out, dx_out = refs[:7]
    scratch = refs[7:]
    me = lax.axis_index("dev")
    orders = bit_orders(n)
    bits = len(orders[0])
    width = sources[0].shape[1]
    groups = [scratch[k * bits:(k + 1) * bits] for k in range(3 * PIECES)]
    inbox, outbox, totals = groups[:PIECES], groups[PIECES:2 * PIECES], groups[2 * PIECES:]
    act_in, dx_in, send, recv, hsend, hrecv = scratch[3 * PIECES * bits:]
    others = greet(n, me, bits)
    up = others[-2]
    halo = [
        remote(act_up, act_in, hsend.at[0], hrecv.at[0], up),
        remote(dx_up, dx_in, hsend.at[1], hrecv.at[1], up),
    ]
    copies = {}

    def bit_at(half, step):
        b = orders[half][bits - 1 - step]
        return b, lax.rem(lax.div(me, 2**b), 2)

    def start(half, step):
        b, bit = bit_at(half, step)
        size = n * BLOCK // 2 ** (step + 1)
        if step == 0:
            src = sources[half].at[pl.ds(pl.multiple_of((1 - bit) * size, BLOCK), size), :]
        else:
            src = outbox[half][step]
        copy = remote(src, inbox[half][step], send.at[half, step], recv.at[half, step], others[b])
        copy.start()
        copies[half, step] = copy

    for half in range(PIECES):
        start(half, 0)
    for copy in halo:
        copy.start()
    for step in range(bits):
        size = n * BLOCK // 2 ** (step + 1)
        for half in range(PIECES):
            copies[half, step].wait_recv()
            _, bit = bit_at(half, step)
            held = sources[half] if step == 0 else totals[half][step - 1]
            base = pl.multiple_of(bit * size, BLOCK)
            if step == bits - 1:
                result[:, half * width:(half + 1) * width] = held[pl.ds(base, size), :].astype(f32) + inbox[half][step][...].astype(f32)
                continue
            _, next_bit = bit_at(half, step + 1)
            part = size // 2
            away = pl.multiple_of((1 - next_bit) * part, BLOCK)
            there = pl.multiple_of(next_bit * part, BLOCK)
            outbox[half][step + 1][...] = (
                held[pl.ds(base + away, part), :].astype(f32)
                + inbox[half][step][pl.ds(away, part), :].astype(f32)
            ).astype(bf16)
            start(half, step + 1)
            totals[half][step][pl.ds(there, part), :] = (
                held[pl.ds(base + there, part), :].astype(f32)
                + inbox[half][step][pl.ds(there, part), :].astype(f32)
            )
    for copy in halo:
        copy.wait_recv()
    act_out[...] = act[...] + act_in[...]
    dx_out[...] = dx[...] + dx_in[...].astype(f32)
    for copy in halo + list(copies.values()):
        copy.wait_send()


def scatter(n, parts, act, act_up, dx, dx_up):
    bits = n.bit_length() - 1
    width = parts[0].shape[1]
    vm = pl.BlockSpec(memory_space=pltpu.VMEM)
    sizes = [n * BLOCK // 2 ** (step + 1) for step in range(bits)]
    boxes = [pltpu.VMEM((size, width), bf16) for size in sizes]
    totals = [pltpu.VMEM((size, width), f32) for size in sizes]
    return pl.pallas_call(
        functools.partial(scatter_kernel, n),
        out_shape=(
            jax.ShapeDtypeStruct((BLOCK, PIECES * width), f32),
            jax.ShapeDtypeStruct(act.shape, act.dtype),
            jax.ShapeDtypeStruct(dx.shape, dx.dtype),
        ),
        in_specs=[vm] * (PIECES + 4),
        out_specs=(vm,) * 3,
        scratch_shapes=boxes * (2 * PIECES) + totals * PIECES + [
            pltpu.VMEM(act.shape, act.dtype),
            pltpu.VMEM(dx.shape, bf16),
            pltpu.SemaphoreType.DMA((PIECES, bits)),
            pltpu.SemaphoreType.DMA((PIECES, bits)),
            pltpu.SemaphoreType.DMA((2,)),
            pltpu.SemaphoreType.DMA((2,)),
        ],
        compiler_params=pltpu.CompilerParams(
            collective_id=1, has_side_effects=True, vmem_limit_bytes=vmem_bytes
        ),
        name="scatter_grads",
    )(*parts, act, act_up, dx, dx_up)


def mm(a, b):
    return jnp.dot(a, b, preferred_element_type=f32)


def mm_nt(a, b):
    return lax.dot_general(a, b, (((1,), (1,)), ((), ())), preferred_element_type=f32)


def mm_tn(a, b):
    return lax.dot_general(a, b, (((0,), (0,)), ((), ())), preferred_element_type=f32)


def norm_forward(x, gain, bias):
    centered = x - jnp.mean(x, axis=-1, keepdims=True)
    inverse = lax.rsqrt(jnp.mean(centered * centered, axis=-1, keepdims=True) + eps_norm)
    hat = centered * inverse
    return (hat * gain + bias).astype(bf16), hat, inverse


def norm_backward(dh, hat, inverse, gain):
    scaled = dh * gain
    dv = inverse * (
        scaled
        - jnp.mean(scaled, axis=-1, keepdims=True)
        - hat * jnp.mean(scaled * hat, axis=-1, keepdims=True)
    )
    return dv, rows_sum(dh * hat), rows_sum(dh)


def rows_sum(x):
    return jnp.sum(x, axis=0, keepdims=True)


def goal_of(c, order, per, layers, l, d):
    inside = c & (BLOCK - 1)
    dev = sum(((c >> (4 + k)) & 1) << b for k, b in enumerate(order))
    row = inside - l * per
    goal = jnp.where((row >= 0) & (row < per), dev * per + row, -1)
    return jnp.where(inside == layers * per + l, d, goal)


def compute_kernel(n, fast, layers, width, hidden_units, ranges, *refs):
    refs = list(refs)
    take = lambda count: [refs.pop(0) for _ in range(count)]
    if fast:
        pieces = take(PIECES)
    else:
        (w_full,) = take(1)
    tok, cot, tok_up, cot_up = take(4)
    if fast:
        parts = take(PIECES)
    else:
        (grad_out,) = take(1)
    act_own, act_up, dx_own, dx_up = take(4)
    w_all, w_one_s, w_two_s, hat1_s, h1_s, qkv_s, p_s, o_s, hat2_s, h2_s, slope_s, a_s = take(12)
    inv_s, dqkv_s, do_s, grad_s, perm = take(5)
    slots = tok.shape[1]
    heads = width // HD
    d = width
    me = lax.axis_index("dev")
    first, last = ranges[me, 0], ranges[me, 1]
    total = ranges[n - 1, 1]
    image = (first + IMG_LEN - 1) // IMG_LEN
    rows = IMAGES_HERE * ROWS

    picks, valid_keys = [], []
    for k in range(IMAGES_HERE):
        begin = (image + k) * IMG_LEN
        count = jnp.where(begin < last, jnp.minimum(IMG_LEN, total - begin), 0)
        r = lax.broadcasted_iota(jnp.int32, (ROWS, 2 * slots), 0)
        c = lax.broadcasted_iota(jnp.int32, (ROWS, 2 * slots), 1)
        t = begin + r
        column = jnp.where(t < last, t - first, t - last + slots)
        column = jnp.where(r < count, column, -1)
        picks.append(jnp.where(column == c, 1.0, 0.0).astype(bf16))
        valid_keys.append(lax.broadcasted_iota(jnp.int32, (ROWS, ROWS), 1) < count)
    pick = jnp.concatenate(picks, axis=0)
    x = mm_nt(pick[:, :slots], tok[...]) + mm_nt(pick[:, slots:], tok_up[...])

    unit = lax.broadcasted_iota(jnp.int32, (1, hidden_units), 1)
    group = sum(jnp.where(unit >= j * d, 1, 0) for j in range(1, 4))
    origin = 4 * (unit - group * d) + group
    f = lax.broadcasted_iota(jnp.int32, (hidden_units, hidden_units), 0)
    perm[...] = jnp.where(f == origin, 1.0, 0.0).astype(bf16)
    if fast:
        place_s, back_s = take(2)
        per = d // n
        orders = bit_orders(n)
        kinds = [orders[:c + 1].index(order) for c, order in enumerate(orders)]
        c = lax.broadcasted_iota(jnp.int32, (1, n * BLOCK), 1)
        line = lax.broadcasted_iota(jnp.int32, (d + BLOCK, n * BLOCK), 0)
        c_down = lax.broadcasted_iota(jnp.int32, (n * BLOCK, 1), 0)
        line_across = lax.broadcasted_iota(jnp.int32, (n * BLOCK, d + BLOCK), 1)
        for kind in sorted(set(kinds)):
            for l in range(layers):
                goal = goal_of(c_down, orders[kind], per, layers, l, d)
                back_s[kind, l] = jnp.where(line_across == goal, 1.0, 0.0).astype(bf16)
                goal = goal_of(c, orders[kind], per, layers, l, d)
                place_s[kind, l] = jnp.where(line == goal, 1.0, 0.0).astype(bf16)

    vec = [None] * layers
    b_one = [None] * layers
    for l in range(layers):
        if fast:
            for c, piece in enumerate(pieces):
                cols = slice(c * piece.shape[1], (c + 1) * piece.shape[1])
                w_all[l, :, cols] = mm(place_s[kinds[c], l], piece[...]).astype(bf16)
        else:
            w_all[l] = w_full[l]
        w_one_s[l] = mm(w_all[l, :d, 4 * d:8 * d], perm[...]).astype(bf16)
        for j in range(4):
            w_two_s[l, j * d:(j + 1) * d, :] = w_all[l, :d, (8 + j) * d:(9 + j) * d]
        tail = w_all[l, d:d + BLOCK, :]
        vec[l] = tail.astype(f32)[0:1, :]
        b_one[l] = mm(tail[:, 8 * d:], perm[...])[0:1, :]

    def v_of(l, index):
        return vec[l][:, index * d:(index + 1) * d]

    for l in range(layers):
        h, hat, inv = norm_forward(x, v_of(l, 0), v_of(l, 1))
        hat1_s[l], h1_s[l], inv_s[l, 0] = hat, h, inv
        projected = mm(h, w_all[l, :d, :3 * d])
        qkv_s[l, :, :d] = ((projected[:, :d] + v_of(l, 2)).astype(bf16).astype(f32)
                           * (1.0 / math.sqrt(HD))).astype(bf16)
        qkv_s[l, :, d:2 * d] = projected[:, d:2 * d].astype(bf16)
        qkv_s[l, :, 2 * d:] = (projected[:, 2 * d:] + v_of(l, 3)).astype(bf16)
        for i in range(IMAGES_HERE):
            at = slice(i * ROWS, (i + 1) * ROWS)
            for head in range(heads):
                q = qkv_s[l, at, head * HD:(head + 1) * HD]
                key = qkv_s[l, at, d + head * HD:d + (head + 1) * HD]
                val = qkv_s[l, at, 2 * d + head * HD:2 * d + (head + 1) * HD]
                scores = jnp.where(valid_keys[i], mm_nt(q, key), masked_fill)
                e = jnp.exp(scores - jnp.max(scores, axis=-1, keepdims=True))
                p = e * (1.0 / jnp.sum(e, axis=-1, keepdims=True))
                p_s[l, i, head] = p
                o_s[l, at, head * HD:(head + 1) * HD] = mm(p.astype(bf16), val).astype(bf16)
        x1 = x + (mm(o_s[l], w_all[l, :d, 3 * d:4 * d]) + v_of(l, 4))
        h2, hat, inv = norm_forward(x1, v_of(l, 5), v_of(l, 6))
        hat2_s[l], h2_s[l], inv_s[l, 1] = hat, h2, inv
        u = mm(h2, w_one_s[l]) + b_one[l]
        phi = 0.5 * (1.0 + lax.erf(u * (1.0 / math.sqrt(2.0))))
        a_s[l] = (u * phi).astype(bf16)
        slope_s[l] = phi + u * (jnp.exp(-0.5 * u * u) * (1.0 / math.sqrt(2.0 * math.pi)))
        x = x1 + (mm(a_s[l], w_two_s[l]) + v_of(l, 7))

    x_low = x.astype(bf16)
    act_own[...] = mm_tn(x_low, pick[:, :slots]).astype(bf16)
    act_up[...] = mm_tn(x_low, pick[:, slots:]).astype(bf16)

    dx = mm_nt(pick[:, :slots], cot[...]) + mm_nt(pick[:, slots:], cot_up[...])
    for l in reversed(range(layers)):
        dm = dx.astype(bf16)
        g_two = mm_tn(a_s[l], dm)
        for j in range(4):
            grad_s[l, :d, (8 + j) * d:(9 + j) * d] = g_two[j * d:(j + 1) * d, :].astype(bf16)
        g_b2 = rows_sum(dm.astype(f32))
        du = (mm_nt(dm, w_two_s[l]) * slope_s[l]).astype(bf16)
        g_b1 = mm_nt(jnp.broadcast_to(rows_sum(du.astype(f32)), (BLOCK, hidden_units)).astype(bf16),
                     perm[...])[0:1, :]
        g_one = mm_tn(h2_s[l], du).astype(bf16)
        grad_s[l, :d, 4 * d:8 * d] = mm_nt(g_one, perm[...]).astype(bf16)
        dh2 = mm_nt(du, w_one_s[l])
        dv, g_g2, g_c2 = norm_backward(dh2, hat2_s[l], inv_s[l, 1], v_of(l, 5))
        dx1 = dx + dv
        db = dx1.astype(bf16)
        g_bo = rows_sum(db.astype(f32))
        grad_s[l, :d, 3 * d:4 * d] = mm_tn(o_s[l], db).astype(bf16)
        do_s[...] = mm_nt(db, w_all[l, :d, 3 * d:4 * d]).astype(bf16)
        for i in range(IMAGES_HERE):
            at = slice(i * ROWS, (i + 1) * ROWS)
            for head in range(heads):
                q_at = slice(head * HD, (head + 1) * HD)
                k_at = slice(d + head * HD, d + (head + 1) * HD)
                v_at = slice(2 * d + head * HD, 2 * d + (head + 1) * HD)
                do = do_s[at, q_at]
                p = p_s[l, i, head]
                dp = mm_nt(do, qkv_s[l, at, v_at])
                ds = (p * (dp - jnp.sum(p * dp, axis=-1, keepdims=True))).astype(bf16)
                dqkv_s[at, q_at] = (mm(ds, qkv_s[l, at, k_at]) * (1.0 / math.sqrt(HD))).astype(bf16)
                dqkv_s[at, k_at] = mm_tn(ds, qkv_s[l, at, q_at]).astype(bf16)
                dqkv_s[at, v_at] = mm_tn(p.astype(bf16), do).astype(bf16)
        g_bq = rows_sum(dqkv_s[:, :d].astype(f32))
        g_bv = rows_sum(dqkv_s[:, 2 * d:].astype(f32))
        grad_s[l, :d, :3 * d] = mm_tn(h1_s[l], dqkv_s[...]).astype(bf16)
        dh = mm_nt(dqkv_s[...], w_all[l, :d, :3 * d])
        dv, g_g1, g_c1 = norm_backward(dh, hat1_s[l], inv_s[l, 0], v_of(l, 0))
        dx = dx1 + dv
        line = jnp.concatenate([g_g1, g_c1, g_bq, g_bv, g_bo, g_g2, g_c2, g_b2, g_b1], axis=1)
        grad_s[l, d:d + BLOCK, :] = jnp.broadcast_to(line, (BLOCK, line.shape[1])).astype(bf16)

    high = dx.astype(bf16)
    low = (dx - high.astype(f32)).astype(bf16)
    dx_own[...] = mm_tn(high, pick[:, :slots]) + mm_tn(low, pick[:, :slots])
    dx_up[...] = mm_tn(high, pick[:, slots:]).astype(bf16)
    if fast:
        for c, out in enumerate(parts):
            cols = slice(c * out.shape[1], (c + 1) * out.shape[1])
            part = mm(back_s[kinds[c], 0], grad_s[0, :, cols])
            for l in range(1, layers):
                part += mm(back_s[kinds[c], l], grad_s[l, :, cols])
            out[...] = part.astype(bf16)
    else:
        grad_out[...] = grad_s[...]


def compute(n, fast, ranges, weights, tok, cot, tok_up, cot_up, layers):
    d, slots = tok.shape
    hidden_units = 4 * d
    rows = IMAGES_HERE * ROWS
    tall = d + BLOCK
    wide = 12 * d
    args = list(weights) + [tok, cot, tok_up, cot_up]
    if fast:
        outs = [jax.ShapeDtypeStruct((n * BLOCK, wide // PIECES), bf16)] * PIECES
        place = [
            pltpu.VMEM((PIECES, layers, tall, n * BLOCK), bf16),
            pltpu.VMEM((PIECES, layers, n * BLOCK, tall), bf16),
        ]
    else:
        outs = [jax.ShapeDtypeStruct((layers, tall, wide), bf16)]
        place = []
    outs += [
        jax.ShapeDtypeStruct((d, slots), kind) for kind in (bf16, bf16, f32, bf16)
    ]
    vm = pl.BlockSpec(memory_space=pltpu.VMEM)
    return pl.pallas_call(
        functools.partial(compute_kernel, n, fast, layers, d, hidden_units),
        out_shape=tuple(outs),
        in_specs=[pl.BlockSpec(memory_space=pltpu.SMEM)] + [vm] * len(args),
        out_specs=(vm,) * len(outs),
        scratch_shapes=[
            pltpu.VMEM((layers, tall, wide), bf16),
            pltpu.VMEM((layers, d, hidden_units), bf16),
            pltpu.VMEM((layers, hidden_units, d), bf16),
            pltpu.VMEM((layers, rows, d), f32),
            pltpu.VMEM((layers, rows, d), bf16),
            pltpu.VMEM((layers, rows, 3 * d), bf16),
            pltpu.VMEM((layers, IMAGES_HERE, d // HD, ROWS, ROWS), f32),
            pltpu.VMEM((layers, rows, d), bf16),
            pltpu.VMEM((layers, rows, d), f32),
            pltpu.VMEM((layers, rows, d), bf16),
            pltpu.VMEM((layers, rows, hidden_units), f32),
            pltpu.VMEM((layers, rows, hidden_units), bf16),
            pltpu.VMEM((layers, 2, rows, 1), f32),
            pltpu.VMEM((rows, 3 * d), bf16),
            pltpu.VMEM((rows, d), bf16),
            pltpu.VMEM((layers, tall, wide), bf16),
            pltpu.VMEM((hidden_units, hidden_units), bf16),
        ] + place,
        compiler_params=pltpu.CompilerParams(vmem_limit_bytes=vmem_bytes),
        name="two_layers",
    )(ranges, *args)


def rows_of(flats, d):
    w_in, w_out, w_one, w_two = flats
    layers = w_in.shape[0]
    return jnp.concatenate(
        [
            w_in.reshape(layers, -1, 3 * d),
            w_out.reshape(layers, -1, d),
            w_one.reshape(layers, -1, 4 * d),
            w_two.reshape(layers, -1, 4 * d),
        ],
        axis=2,
    )


def flats_of(block, d):
    layers = block.shape[0]
    ends = (0, 3 * d, 4 * d, 8 * d, 12 * d)
    return [block[:, :, lo:hi].reshape(layers, -1) for lo, hi in zip(ends, ends[1:])]


def local(tokens, ranges, attn_in, attn_out, mlp_in, mlp_out, vectors, cotangent):
    n = lax.axis_size("dev")
    me = lax.axis_index("dev")
    slots, d = tokens.shape
    layers, part = vectors.shape
    tokens, cotangent = tokens.T, cotangent.T
    flats = (attn_in, attn_out, mlp_in, mlp_out)
    fast = d % n == 0 and n & (n - 1) == 0 and layers * (d // n + 1) <= BLOCK and n >= 32
    if fast:
        per = d // n
        block = rows_of(flats, d).reshape(layers * per, 12 * d)
        line = jnp.zeros((layers, 12 * d), bf16)
        line = lax.dynamic_update_slice(line, vectors, (0, me * part))
        spare = jnp.zeros((BLOCK - layers * (per + 1), 12 * d), bf16)
        block = jnp.concatenate([block, line, spare], axis=0)
        *pieces, tok_up, cot_up = gather(n, block, tokens, cotangent)
        *parts, act, act_up, dx, dx_up = compute(
            n, True, ranges, pieces, tokens, cotangent, tok_up, cot_up, layers
        )
        full, act, dx = scatter(n, parts, act, act_up, dx, dx_up)
        grads = flats_of(full[:layers * per].reshape(layers, per, 12 * d), d)
        lines = full[layers * per:layers * (per + 1)]
        grads.append(lax.dynamic_slice(lines, (0, me * part), (layers, part)))
    else:
        whole = [
            jnp.stack([lax.all_gather(flat[l], "dev", axis=0, tiled=True) for l in range(layers)])
            for flat in flats + (vectors,)
        ]
        line = whole.pop()
        spare = jnp.zeros((layers, BLOCK - 1, 12 * d), bf16)
        block = jnp.concatenate([rows_of(whole, d), line[:, None, :], spare], axis=1)
        down = [(i, (i + n - 1) % n) for i in range(n)]
        tok_up, cot_up = lax.ppermute(tokens, "dev", down), lax.ppermute(cotangent, "dev", down)
        grad, act, act_up, dx, dx_up = compute(
            n, False, ranges, (block,), tokens, cotangent, tok_up, cot_up, layers
        )
        up = [(i, (i + 1) % n) for i in range(n)]
        act = act + lax.ppermute(act_up, "dev", up)
        dx = dx + lax.ppermute(dx_up, "dev", up)
        terms = flats_of(grad[:, :d], d) + [grad[:, d]]
        grads = [
            jnp.stack([
                lax.psum_scatter(term[l].astype(f32), "dev", scatter_dimension=0, tiled=True)
                for l in range(layers)
            ])
            for term in terms
        ]
    return (act.T, dx.T, *grads)


def solution(mesh):
    flat = P(None, "dev")
    rows = P("dev", None)
    return jax.shard_map(
        local,
        mesh=mesh,
        in_specs=(rows, P(), flat, flat, flat, flat, flat, rows),
        out_specs=(rows, rows, flat, flat, flat, flat, flat),
        check_vma=False,
    )
```

profile of v0, /device:TPU:0, one launch (start us, length us, event | category | flops | bytes accessed | tf_op | source)
XLA Modules:
  0.0 84.8 jit_solution(18176519619991838379)
XLA Ops:
  0.6 0.0 copy-start.5
  0.6 0.7 copy-done.5
  1.3 0.0 copy-start.7
  1.3 0.0 copy-start.6
  1.3 0.1 concatenate.16
  1.4 0.0 copy-start.4
  1.4 0.5 copy-done.7
  2.0 0.1 dynamic_update_slice.3
  2.1 0.0 copy-done.6
  2.1 0.7 copy.16.ranges
  2.8 0.0 copy-done.4
  2.8 0.1 concatenate.15
  2.9 0.6 copy-done.2
  3.5 0.7 copy-done.3
  4.2 0.1 concatenate.19
  4.3 0.7 pad_maximum_fusion.blk
  5.0 25.6 %gather_params.1 = (bf16[512,384]{1,0:T(8,128)(2,1)}, bf16[512,384]{1,0:T(8,128)(2,1)}, bf16[512,384]{1,0:T(8,128)(2,1)}, bf16[512,384]{1,0:T(8,128)(2,1)}, bf16...) custom-call(bf16[16,2304]{1,0:T(8,128)(2,1)} %pad_maximum_fusion.blk, ...), custom_call_target="tpu_custom_call" | custom-call | tf_op jit(solution)/shard_map/gather_params/pallas_call | solution.py:98
  30.6 22.6 %two_layers.1 = (bf16[512,384]{1,0:T(8,128)(2,1)}, bf16[512,384]{1,0:T(8,128)(2,1)}, bf16[512,384]{1,0:T(8,128)(2,1)}, bf16[512,384]{1,0:T(8,128)(2,1)}, bf16[51...) custom-call(s32[32,2]{1,0:T(8,128)} %copy.16.ranges, ...), custom_call_target="tpu_custom_call" | custom-call | tf_op jit(solution)/shard_map/two_layers/pallas_call | solution.py:444
  53.2 25.0 %scatter_grads.1 = (f32[16,2304]{1,0:T(8,128)}, bf16[192,256]{1,0:T(8,128)(2,1)}, f32[192,256]{1,0:T(8,128)}) custom-call(bf16[512,384]{1,0:T(8,128)(2,1)} %get-tuple-element.36.refs_0_, bf16[512,384]{1,0:T(8,128)(2,1)} %get-tuple-element.37.refs_1_, bf16[512,384]{1,0:T(8,128)(2,1)} %get-tuple-element.38.refs_2_, ...), custom_call_target="tpu_custom_call" | custom-call | tf_op jit(solution)/shard_map/scatter_grads/pallas_call | solution.py:193
  78.2 0.9 %slice.23 = f32[2,2304]{1,0:T(2,128)S(1)} slice(f32[16,2304]{1,0:T(8,128)} %get-tuple-element.48), slice={[12:14], [0:2304]} | slice | bytes 36864 | tf_op jit(solution)/shard_map/slice | solution.py:514
  79.1 0.6 constant_dynamic-slice_fusion
  79.8 0.9 %reshape.42 = f32[2,6,2304]{2,1,0:T(8,128)S(1)} reshape(f32[12,2304]{1,0:T(8,128)} %bitcast.16) | data formatting | bytes 221184 | tf_op jit(solution)/shard_map/reshape | solution.py:513
  80.7 0.1 slice.25
  80.8 0.7 reshape.44
  81.5 0.0 copy-start.1
  81.5 0.7 reshape.43
  82.2 0.6 copy.18
  82.8 0.6 copy.17
  83.5 0.0 copy-done.1
  83.5 0.6 copy.22
  84.1 0.0 copy-done
  84.1 0.7 copy.23
  (9 shorter events, 0.1 us)
Async XLA Ops:
  0.6 0.7 copy-start.5
  1.3 0.7 copy-start.7
  1.3 0.7 copy-start.6
  1.4 1.4 %copy-start.4 = (bf16[2,3456]{1,0:T(2,128)(2,1)S(1)}, bf16[2,3456]{1,0:T(2,128)(2,1)}, u32[]{:S(2)}) copy-start(bf16[2,3456]{1,0:T(2,128)(2,1)} %param.10) | copy-start | bytes 41476
  2.8 0.7 copy-start.2
  3.5 0.7 copy-start.3
  81.5 2.0 %copy-start.1 = (bf16[192,256]{1,0:T(8,128)(2,1)S(1)}, bf16[192,256]{1,0:T(8,128)(2,1)}, u32[]{:S(2)}) copy-start(bf16[192,256]{1,0:T(8,128)(2,1)} %get-tuple-element.46) | copy-start | bytes 294916
  82.2 1.9 %copy-start = (f32[192,256]{1,0:T(8,128)S(1)}, f32[192,256]{1,0:T(8,128)}, u32[]{:S(2)}) copy-start(f32[192,256]{1,0:T(8,128)} %get-tuple-element.47) | copy-start | bytes 589828
where the time goes:
time: 85.3 us; the launch traced here: 84.8 us
  Pallas kernels  73.2 us (86%)
  local copies, waits for them, and re-layouts  10.2 us (12%)
    pallas_call x1, Pallas kernels, gather(): pl.pallas_call(functools.partial(gather_kernel, n), out_shape=(jax.ShapeD...  25.6 us
    pallas_call x1, Pallas kernels, scatter(): pl.pallas_call(functools.partial(scatter_kernel, n), out_shape=(jax.Shape...  25 us
    pallas_call x1, Pallas kernels, compute(): pl.pallas_call(functools.partial(compute_kernel, n, fast, layers, d, hidd...  22.6 us
    unnamed x22, local copies, waits for them, and re-layouts  5.86 us

commit v1 on v0

v1 whole, which is shorter than its diff:
```python
import functools
import math

import jax
import jax.numpy as jnp
from jax import lax
from jax.experimental import pallas as pl
from jax.experimental.pallas import tpu as pltpu
from jax.sharding import PartitionSpec as P

HD = 64
IMG_LEN = 197
ROWS = 208
IMAGES_HERE = 2
BLOCK = 16
MESH_ID = pl.DeviceIdType.MESH
bf16, f32 = jnp.bfloat16, jnp.float32
eps_norm = 1e-06
masked_fill = -1e30
vmem_bytes = 56 * 2**20


def mm(a, b):
    return jnp.dot(a, b, preferred_element_type=f32)


def mm_nt(a, b):
    return lax.dot_general(a, b, (((1,), (1,)), ((), ())), preferred_element_type=f32)


def mm_tn(a, b):
    return lax.dot_general(a, b, (((0,), (0,)), ((), ())), preferred_element_type=f32)


def norm_forward(x, gain, bias):
    centered = x - jnp.mean(x, axis=-1, keepdims=True)
    inverse = lax.rsqrt(jnp.mean(centered * centered, axis=-1, keepdims=True) + eps_norm)
    hat = centered * inverse
    return (hat * gain + bias).astype(bf16), hat, inverse


def norm_backward(dh, hat, inverse, gain):
    scaled = dh * gain
    dv = inverse * (
        scaled
        - jnp.mean(scaled, axis=-1, keepdims=True)
        - hat * jnp.mean(scaled * hat, axis=-1, keepdims=True)
    )
    return dv, rows_sum(dh * hat), rows_sum(dh)


def rows_sum(x):
    return jnp.sum(x, axis=0, keepdims=True)


WAYS = 3


def remote(src, dst, send, recv, dev):
    return pltpu.make_async_remote_copy(
        src_ref=src, dst_ref=dst, send_sem=send, recv_sem=recv,
        device_id=(dev,), device_id_type=MESH_ID,
    )


class Place:
    def __init__(self, n):
        self.n = n
        me = self.me = lax.axis_index("dev")
        self.bits = [lax.rem(lax.div(me, 2**b), 2) for b in range(5)]
        self.c, self.x, self.y = self.bits[:3]
        self.z = lax.div(me, 8)
        self.core = self.flip(0)
        self.along_z = [self.flip(3), self.flip(4), self.flip(3, 4)]
        self.along_xy = [self.flip(1), self.flip(2), self.flip(1, 2)]
        self.up, self.down = lax.rem(me + 1, n), lax.rem(me + n - 1, n)

    def flip(self, *which):
        return self.me + sum((1 - 2 * self.bits[b]) * 2**b for b in which)

    def peers(self):
        return [self.core] + self.along_z + self.along_xy + [self.up, self.down]


class Gather:
    def __init__(self, place, buf, send, recv):
        self.place, self.buf, self.send, self.recv = place, buf, send, recv
        self.sent = []

    def go(self, at, dev):
        k = len(self.sent)
        copy = remote(at, at, self.send.at[k], self.recv.at[k], dev)
        copy.start()
        self.sent.append(copy)

    def begin(self):
        p = self.place
        for dev in p.along_z:
            self.go(self.buf.at[p.z, p.y, p.x, p.c], dev)

    def middle(self):
        p = self.place
        for copy in self.sent[:WAYS]:
            copy.wait_recv()
        for dev in p.along_xy:
            self.go(self.buf.at[:, p.y, p.x, p.c], dev)

    def core(self):
        p = self.place
        for copy in self.sent[WAYS:2 * WAYS]:
            copy.wait_recv()
        self.go(self.buf.at[:, :, :, p.c], p.core)

    def done(self):
        self.sent[-1].wait_recv()


class Scatter:
    def __init__(self, place, grads, half, mid, ours, last, send, recv, out):
        self.place, self.grads, self.half, self.mid = place, grads, half, mid
        self.ours, self.last, self.send, self.recv, self.out = ours, last, send, recv, out
        self.out_xy, self.in_xy = mid
        self.out_z, self.in_z = last
        self.sent = []

    def go(self, src, dst, dev):
        k = len(self.sent)
        copy = remote(src, dst, self.send.at[k], self.recv.at[k], dev)
        copy.start()
        self.sent.append(copy)

    def begin(self):
        p = self.place
        self.go(self.grads.at[:, :, :, 1 - p.c], self.half, p.core)

    def middle(self):
        p = self.place
        self.sent[0].wait_recv()
        self.out_xy[...] = (
            self.grads[:, :, :, p.c].astype(f32) + self.half[...].astype(f32)
        ).astype(bf16)
        for k, (dy, dx) in enumerate(((0, 1), (1, 0), (1, 1))):
            y = 1 - p.y if dy else p.y
            x = 1 - p.x if dx else p.x
            self.go(self.out_xy.at[:, y, x], self.in_xy.at[k], p.along_xy[k])

    def end(self):
        p = self.place
        for copy in self.sent[1:1 + WAYS]:
            copy.wait_recv()
        total = self.grads[:, p.y, p.x, p.c].astype(f32) + self.half[:, p.y, p.x].astype(f32)
        for k in range(WAYS):
            total += self.in_xy[k].astype(f32)
        self.ours[...] = total
        self.out_z[...] = total.astype(bf16)
        for k, dev in enumerate(p.along_z):
            self.go(self.out_z.at[lax.div(dev, 8)], self.in_z.at[k], dev)

    def done(self):
        for copy in self.sent[1 + WAYS:]:
            copy.wait_recv()
        total = self.ours[self.place.z]
        for k in range(WAYS):
            total += self.in_z[k].astype(f32)
        self.out[...] = total


def natural(c):
    return jnp.where((c & 7) < 6, 6 * (c >> 3) + (c & 7), -1)


def iota(shape, dim):
    return lax.broadcasted_iota(jnp.int32, shape, dim)


def norm_padded(x, gain, bias, real, d):
    centered = (x - jnp.sum(x, axis=-1, keepdims=True) * (1.0 / d)) * real
    inverse = lax.rsqrt(jnp.sum(centered * centered, axis=-1, keepdims=True) * (1.0 / d) + eps_norm)
    hat = centered * inverse
    return (hat * gain + bias).astype(bf16), hat, inverse


def norm_padded_back(dh, hat, inverse, gain, d):
    scaled = dh * gain
    dv = inverse * (
        scaled
        - jnp.sum(scaled, axis=-1, keepdims=True) * (1.0 / d)
        - hat * (jnp.sum(scaled * hat, axis=-1, keepdims=True) * (1.0 / d))
    )
    return dv, rows_sum(dh * hat), rows_sum(dh)


def fused_kernel(n, layers, d, ranges, *refs):
    refs = list(refs)
    take = lambda count: [refs.pop(0) for _ in range(count)]
    tok, cot, a_in, a_out, m_in, m_out, vecs = take(7)
    red_i, red_m, red_o, act_out, dx_out = take(5)
    wire_i, wire_m, wire_o = take(3)
    grad_i, grad_m, grad_o = take(3)
    half_i, half_m, half_o = take(3)
    mid_i, mid_m, mid_o = take(3)
    inxy_i, inxy_m, inxy_o = take(3)
    ours_i, ours_m, ours_o = take(3)
    outz_i, outz_m, outz_o = take(3)
    inz_i, inz_m, inz_o = take(3)
    tok_up, cot_up, act_up, act_in, dx_up, dx_in = take(6)
    w_in_s, w_one_s, w_out_s, w_two_s = take(4)
    hat1_s, h1_s, qkv_s, p_s, o_s, hat2_s, h2_s, slope_s, a_s, inv_s = take(10)
    dqkv_s, do_s, stage, flat_ai, flat_ao, flat_mi, flat_mo, vec_s = take(8)
    gsend, grecv, ssend, srecv, hsend, hrecv = take(6)
    slots = tok.shape[1]
    heads = d // HD
    wide = 8 * n
    hidden_units = 4 * d
    rows = IMAGES_HERE * ROWS
    place = Place(n)
    me = place.me

    barrier = pltpu.get_barrier_semaphore()
    for other in place.peers():
        pl.semaphore_signal(barrier, inc=1, device_id=(other,), device_id_type=MESH_ID)

    lane = iota((1, wide), 1)
    real = jnp.where((lane & 7) < 6, 1.0, 0.0)
    ones_lane = jnp.where((lane & 7) == 6, 1.0, 0.0)
    spread = jnp.where(iota((d, wide), 0) == natural(iota((1, wide), 1)), 1.0, 0.0).astype(bf16)

    part = vecs.shape[1]
    vec_s[...] = jnp.zeros_like(vec_s)
    vec_s[0:layers, 0:part] = vecs[...].astype(f32)
    columns = 8 * d + hidden_units
    pick_vec = jnp.where(
        iota((vec_s.shape[1], columns), 0) == iota((1, columns), 1) - part * me, 1.0, 0.0
    ).astype(bf16)
    lines = mm(vec_s[...].astype(bf16), pick_vec)
    flat_ai[...] = a_in[...].astype(f32)
    flat_ao[...] = a_out[...].astype(f32)
    flat_mi[...] = m_in[...].astype(f32)
    flat_mo[...] = m_out[...].astype(f32)
    here = (place.z, place.y, place.x, place.c)
    big, small = stage
    for l in range(layers):
        row = slice(l, l + 1)
        small[...] = jnp.zeros_like(small)
        for r in range(6):
            small[r:r + 1, :] = flat_ao[row, r * d:(r + 1) * d]
        for r in range(24):
            small[8 + r:9 + r, :] = flat_mo[row, r * d:(r + 1) * d]
        for r, block in ((6, 4), (32, 0), (33, 1), (34, 5), (35, 6), (36, 7)):
            small[r:r + 1, :] = lines[row, block * d:(block + 1) * d]
        padded = mm(small[...].astype(bf16), spread)
        wire_o[(l,) + here] = padded[:32].astype(bf16)
        big[0] = jnp.zeros_like(big[0])
        big[1] = jnp.zeros_like(big[1])
        for r in range(6):
            big[0, r:r + 1, :] = flat_ai[row, r * 3 * d:r * 3 * d + 2 * d]
            big[0, 8 + r:9 + r, :d] = flat_ai[row, r * 3 * d + 2 * d:(r + 1) * 3 * d]
            big[1, r:r + 1, :] = flat_mi[row, r * 4 * d:r * 4 * d + 2 * d]
            big[1, 8 + r:9 + r, :] = flat_mi[row, r * 4 * d + 2 * d:(r + 1) * 4 * d]
        big[0, 6:7, :d] = lines[row, 2 * d:3 * d]
        big[0, 14:15, :d] = lines[row, 3 * d:4 * d]
        big[0, 7:8, :wide] = padded[32:33]
        big[0, 15:16, :wide] = padded[33:34]
        big[1, 6:7, :] = lines[row, 8 * d:10 * d]
        big[1, 14:15, :] = lines[row, 10 * d:12 * d]
        big[1, 7:8, :wide] = padded[34:35]
        big[1, 7:8, wide:] = padded[35:36, :2 * d - wide]
        big[1, 15:16, :2 * wide - 2 * d] = padded[35:36, 2 * d - wide:]
        big[1, 15:16, 2 * wide - 2 * d:] = padded[36:37]
        wire_i[(l,) + here] = big[0].astype(bf16)
        wire_m[(l,) + here] = big[1].astype(bf16)

    wires = (wire_i, wire_m, wire_o)
    gathers = [
        [Gather(place, wires[k].at[l], gsend.at[l, k], grecv.at[l, k]) for k in range(3)]
        for l in range(layers)
    ]
    scatters = [
        [
            Scatter(
                place, grads.at[l], half.at[l], (mid.at[l], inxy.at[l]), ours.at[l],
                (outz.at[l], inz.at[l]), ssend.at[l, k], srecv.at[l, k], red.at[l],
            )
            for k, (grads, half, mid, inxy, ours, outz, inz, red) in enumerate((
                (grad_i, half_i, mid_i, inxy_i, ours_i, outz_i, inz_i, red_i),
                (grad_m, half_m, mid_m, inxy_m, ours_m, outz_m, inz_m, red_m),
                (grad_o, half_o, mid_o, inxy_o, ours_o, outz_o, inz_o, red_o),
            ))
        ]
        for l in range(layers)
    ]
    halo = [
        remote(tok, tok_up, hsend.at[0], hrecv.at[0], place.down),
        remote(cot, cot_up, hsend.at[1], hrecv.at[1], place.down),
        remote(act_up, act_in, hsend.at[2], hrecv.at[2], place.up),
        remote(dx_up, dx_in, hsend.at[3], hrecv.at[3], place.up),
    ]
    (gi0, gm0, go0), (gi1, gm1, go1) = gathers
    (si0, sm0, so0), (si1, sm1, so1) = scatters

    pl.semaphore_wait(barrier, len(place.peers()))
    gi0.begin()
    halo[0].start()

    first, last = ranges[0, me], ranges[1, me]
    total = ranges[1, n - 1]
    image = (first + IMG_LEN - 1) // IMG_LEN
    picks, valid_keys = [], []
    for k in range(IMAGES_HERE):
        begin = (image + k) * IMG_LEN
        count = jnp.where(begin < last, jnp.minimum(IMG_LEN, total - begin), 0)
        r = iota((ROWS, 2 * slots), 0)
        c = iota((ROWS, 2 * slots), 1)
        t = begin + r
        column = jnp.where(t < last, t - first, t - last + slots)
        column = jnp.where(r < count, column, -1)
        picks.append(jnp.where(column == c, 1.0, 0.0).astype(bf16))
        valid_keys.append(iota((ROWS, ROWS), 1) < count)
    pick = jnp.concatenate(picks, axis=0)
    x = mm_nt(pick[:, :slots], mm_tn(spread, tok[...]).astype(bf16))

    gi0.middle()
    go0.begin()
    gm0.begin()
    halo[0].wait_recv()
    x += mm_nt(pick[:, slots:], mm_tn(spread, tok_up[...]).astype(bf16))
    gi0.core()
    go0.middle()
    gm0.middle()
    gi1.begin()
    halo[1].start()

    def unpack_in(l):
        v = wire_i[l].reshape(2 * n * 8, 2 * d).astype(f32).reshape(n, 2, 8, 2 * d)
        w_in_s[l, :, :2 * d] = v[:, 0].reshape(wide, 2 * d).astype(bf16)
        w_in_s[l, :, 2 * d:] = v[:, 1].reshape(wide, 2 * d).astype(bf16)
        s = jnp.sum(v, axis=0)
        return s[0, 7:8, :wide], s[1, 7:8, :wide] + ones_lane

    def unpack_one(l):
        v = wire_m[l].reshape(2 * n * 8, 2 * d).astype(f32).reshape(n, 2, 8, 2 * d)
        w_one_s[l, :, :2 * d] = v[:, 0].reshape(wide, 2 * d).astype(bf16)
        w_one_s[l, :, 2 * d:] = v[:, 1].reshape(wide, 2 * d).astype(bf16)
        s = jnp.sum(v, axis=0)
        bias = jnp.concatenate([s[0, 7:8, wide:], s[1, 7:8, :2 * wide - 2 * d]], axis=1)
        return s[0, 7:8, :wide], bias + ones_lane, s[1, 7:8, 2 * wide - 2 * d:]

    def unpack_out(l):
        v = wire_o[l].reshape(4 * n * 8, wide).astype(f32).reshape(n, 4, 8, wide)
        w_out_s[l] = mm(spread, v[:, 0].reshape(wide, wide).astype(bf16)).astype(bf16)
        w_two_s[l] = v[:, 1:].reshape(hidden_units, wide).astype(bf16)
        return jnp.sum(v[:, 0], axis=0)[6:7, :]

    gain1, gain2 = [None] * layers, [None] * layers
    beats = [
        [lambda: (go0.core(), gi1.middle()), lambda: (gm0.core(), go1.begin(), gm1.begin()),
         lambda: gi1.core(), lambda: (go1.middle(), gm1.middle())],
        [lambda: go1.core(), lambda: gm1.core(), lambda: None, lambda: None],
    ]
    for l in range(layers):
        gi, gm, go = gathers[l]
        gi.done()
        gain1[l], bias = unpack_in(l)
        h, hat, inv = norm_padded(x, gain1[l], bias, real, d)
        hat1_s[l], h1_s[l], inv_s[l, 0] = hat, h, inv
        projected = mm(h, w_in_s[l, :, :3 * d])
        qkv_s[l, :, :d] = (projected[:, :d].astype(bf16).astype(f32)
                           * (1.0 / math.sqrt(HD))).astype(bf16)
        qkv_s[l, :, d:] = projected[:, d:].astype(bf16)
        beats[l][0]()
        for i in range(IMAGES_HERE):
            at = slice(i * ROWS, (i + 1) * ROWS)
            for head in range(heads):
                q = qkv_s[l, at, head * HD:(head + 1) * HD]
                key = qkv_s[l, at, d + head * HD:d + (head + 1) * HD]
                val = qkv_s[l, at, 2 * d + head * HD:2 * d + (head + 1) * HD]
                scores = jnp.where(valid_keys[i], mm_nt(q, key), masked_fill)
                e = jnp.exp(scores - jnp.max(scores, axis=-1, keepdims=True))
                p = e * (1.0 / jnp.sum(e, axis=-1, keepdims=True))
                p_s[l, i, head] = p
                o_s[l, at, head * HD:(head + 1) * HD] = mm(p.astype(bf16), val).astype(bf16)
            beats[l][1 + i]()
        go.done()
        b_out = unpack_out(l)
        x1 = x + (mm(o_s[l], w_out_s[l]) + b_out)
        gm.done()
        gain2[l], bias, b_two = unpack_one(l)
        h2, hat, inv = norm_padded(x1, gain2[l], bias, real, d)
        hat2_s[l], h2_s[l], inv_s[l, 1] = hat, h2, inv
        u = mm(h2, w_one_s[l])
        beats[l][3]()
        phi = 0.5 * (1.0 + lax.erf(u * (1.0 / math.sqrt(2.0))))
        a_s[l] = (u * phi).astype(bf16)
        slope_s[l] = phi + u * (jnp.exp(-0.5 * u * u) * (1.0 / math.sqrt(2.0 * math.pi)))
        x = x1 + (mm(a_s[l], w_two_s[l]) + b_two)

    x_low = mm_nt(x.astype(bf16), spread).astype(bf16)
    act_up[...] = mm_tn(x_low, pick[:, slots:]).astype(bf16)
    halo[2].start()
    act_own = mm_tn(x_low, pick[:, :slots]).astype(bf16)

    halo[1].wait_recv()
    dx = mm_nt(pick[:, :slots], mm_tn(spread, cot[...]).astype(bf16))
    dx += mm_nt(pick[:, slots:], mm_tn(spread, cot_up[...]).astype(bf16))

    row_of = iota((wide, 1), 0) & 7

    def fold(a, b):
        v = jnp.concatenate([a.reshape(n, 1, 8, 2 * d), b.reshape(n, 1, 8, 2 * d)], axis=1)
        return v.reshape(2 * n * 8, 2 * d).astype(bf16).reshape(4, 2, 2, 2, BLOCK, 2 * d)

    beats = [
        [lambda: (so1.end(), si1.middle()), lambda: (si1.end(), so1.done()),
         lambda: (sm0.middle(), si1.done()), lambda: so0.middle(), lambda: sm0.end()],
        [lambda: None, lambda: None, lambda: sm1.middle(), lambda: so1.middle(), lambda: (sm1.end())],
    ]
    spare = jnp.zeros((rows, d), bf16)
    for l in reversed(range(layers)):
        si, sm, so = scatters[l]
        dm = dx.astype(bf16)
        g_b2 = rows_sum(dm.astype(f32))
        du = (mm_nt(dm, w_two_s[l]) * slope_s[l]).astype(bf16)
        beats[l][0]()
        g_one = mm_tn(h2_s[l], du)
        dh2 = mm_nt(du, w_one_s[l])
        dv, g_g2, g_c2 = norm_padded_back(dh2, hat2_s[l], inv_s[l, 1], gain2[l], d)
        line = jnp.concatenate([g_g2, g_c2, g_b2], axis=1)
        g_one = jnp.where(row_of == 7, line, g_one)
        grad_m[l] = fold(g_one[:, :2 * d], g_one[:, 2 * d:])
        sm.begin()
        dx1 = dx + dv
        db = dx1.astype(bf16)
        g_bo = rows_sum(db.astype(f32))
        do_s[...] = mm_nt(db, w_out_s[l]).astype(bf16)
        beats[l][1]()
        g_two = mm_tn(a_s[l], dm)
        g_out = mm_tn(spread, mm_tn(o_s[l], db).astype(bf16))
        g_out = jnp.where(row_of == 6, g_bo, g_out)
        v = jnp.concatenate([g_out.reshape(n, 1, 8, wide), g_two.reshape(n, 3, 8, wide)], axis=1)
        grad_o[l] = v.reshape(4 * n * 8, wide).astype(bf16).reshape(4, 2, 2, 2, 2 * BLOCK, wide)
        so.begin()
        beats[l][2]()
        dqkv_s[:, 3 * d:] = spare
        for i in range(IMAGES_HERE):
            at = slice(i * ROWS, (i + 1) * ROWS)
            for head in range(heads):
                q_at = slice(head * HD, (head + 1) * HD)
                k_at = slice(d + head * HD, d + (head + 1) * HD)
                v_at = slice(2 * d + head * HD, 2 * d + (head + 1) * HD)
                do = do_s[at, q_at]
                p = p_s[l, i, head]
                dp = mm_nt(do, qkv_s[l, at, v_at])
                ds = (p * (dp - jnp.sum(p * dp, axis=-1, keepdims=True))).astype(bf16)
                dqkv_s[at, q_at] = (mm(ds, qkv_s[l, at, k_at]) * (1.0 / math.sqrt(HD))).astype(bf16)
                dqkv_s[at, k_at] = mm_tn(ds, qkv_s[l, at, q_at]).astype(bf16)
                dqkv_s[at, v_at] = mm_tn(p.astype(bf16), do).astype(bf16)
            beats[l][3 + i]()
        dh = mm_nt(dqkv_s[...], w_in_s[l])
        dv, g_g1, g_c1 = norm_padded_back(dh, hat1_s[l], inv_s[l, 0], gain1[l], d)
        g_in = mm_tn(h1_s[l], dqkv_s[...])
        blank = jnp.zeros((1, 2 * d - wide), f32)
        line = jnp.concatenate([g_g1, blank, g_c1, blank], axis=1)
        g_in = jnp.where(row_of == 7, line, g_in)
        grad_i[l] = fold(g_in[:, :2 * d], g_in[:, 2 * d:])
        si.begin()
        dx = dx1 + dv

    high = dx.astype(bf16)
    low = (dx - high.astype(f32)).astype(bf16)
    high = mm_nt(high, spread).astype(bf16)
    low = mm_nt(low, spread).astype(bf16)
    dx_up[...] = mm_tn(high, pick[:, slots:]).astype(bf16)
    halo[3].start()
    so0.end()
    si0.middle()
    sm0.done()
    dx_own = mm_tn(high, pick[:, :slots]) + mm_tn(low, pick[:, :slots])
    sm1.done()
    so0.done()
    si0.end()
    halo[2].wait_recv()
    act_out[...] = act_own + act_in[...]
    halo[3].wait_recv()
    dx_out[...] = dx_own + dx_in[...].astype(f32)
    si0.done()
    for copy in halo:
        copy.wait_send()
    for group in gathers + scatters:
        for each in group:
            for copy in each.sent:
                copy.wait_send()


def fused(n, ranges, tok, cot, flats):
    d, slots = tok.shape
    layers = flats[0].shape[0]
    wide = 8 * n
    hidden_units = 4 * d
    rows = IMAGES_HERE * ROWS
    shapes = ((BLOCK, 2 * d), (BLOCK, 2 * d), (2 * BLOCK, wide))
    boxes = lambda lead, kind: [pltpu.VMEM((layers,) + lead + s, kind) for s in shapes]
    vm = pl.BlockSpec(memory_space=pltpu.VMEM)
    scratch = (
        boxes((4, 2, 2, 2), bf16) + boxes((4, 2, 2, 2), bf16)
        + boxes((4, 2, 2), bf16) + boxes((4, 2, 2), bf16) + boxes((WAYS, 4), bf16)
        + boxes((4,), f32) + boxes((4,), bf16) + boxes((WAYS,), bf16)
        + [pltpu.VMEM((d, slots), bf16)] * 6
        + [
            pltpu.VMEM((layers, wide, 4 * d), bf16),
            pltpu.VMEM((layers, wide, hidden_units), bf16),
            pltpu.VMEM((layers, d, wide), bf16),
            pltpu.VMEM((layers, hidden_units, wide), bf16),
            pltpu.VMEM((layers, rows, wide), f32),
            pltpu.VMEM((layers, rows, wide), bf16),
            pltpu.VMEM((layers, rows, 3 * d), bf16),
            pltpu.VMEM((layers, IMAGES_HERE, d // HD, ROWS, ROWS), f32),
            pltpu.VMEM((layers, rows, d), bf16),
            pltpu.VMEM((layers, rows, wide), f32),
            pltpu.VMEM((layers, rows, wide), bf16),
            pltpu.VMEM((layers, rows, hidden_units), f32),
            pltpu.VMEM((layers, rows, hidden_units), bf16),
            pltpu.VMEM((layers, 2, rows, 1), f32),
            pltpu.VMEM((rows, 4 * d), bf16),
            pltpu.VMEM((rows, d), bf16),
            (pltpu.VMEM((2, BLOCK, 2 * d), f32), pltpu.VMEM((3 * BLOCK, d), f32)),
        ]
        + [pltpu.VMEM(f.shape, f32) for f in flats[:4]]
        + [pltpu.VMEM((BLOCK, 128), f32)]
        + [pltpu.SemaphoreType.DMA((layers, 3, 2 * WAYS + 1))] * 4
        + [pltpu.SemaphoreType.DMA((4,))] * 2
    )
    return pl.pallas_call(
        functools.partial(fused_kernel, n, layers, d),
        out_shape=tuple(jax.ShapeDtypeStruct((layers,) + s, f32) for s in shapes)
        + (jax.ShapeDtypeStruct((d, slots), bf16), jax.ShapeDtypeStruct((d, slots), f32)),
        in_specs=[pl.BlockSpec(memory_space=pltpu.SMEM)] + [vm] * 7,
        out_specs=(vm,) * 5,
        scratch_shapes=scratch,
        compiler_params=pltpu.CompilerParams(
            collective_id=0, has_side_effects=True, vmem_limit_bytes=vmem_bytes
        ),
        name="two_layers",
    )(ranges.T, tok, cot, *flats)


def split_mm_nt(a, b):
    high = a.astype(bf16)
    low = (a - high.astype(f32)).astype(bf16)
    return mm_nt(high, b) + mm_nt(low, b)


def flatten_kernel(n, layers, d, red_i, red_m, red_o, act_in, dx_in, act, dx, g_in, g_out, g_one, g_two, g_vec, line_s, out_s):
    me = lax.axis_index("dev")
    wide = 8 * n
    act[...] = act_in[...]
    dx[...] = dx_in[...]
    spread = jnp.where(iota((d, wide), 0) == natural(iota((1, wide), 1)), 1.0, 0.0).astype(bf16)
    line_s[...] = jnp.zeros_like(line_s)
    for l in range(layers):
        row = slice(l, l + 1)
        for r in range(6):
            g_in[row, r * 3 * d:r * 3 * d + 2 * d] = red_i[l, r:r + 1, :]
            g_in[row, r * 3 * d + 2 * d:(r + 1) * 3 * d] = red_i[l, 8 + r:9 + r, :d]
            g_one[row, r * 4 * d:r * 4 * d + 2 * d] = red_m[l, r:r + 1, :]
            g_one[row, r * 4 * d + 2 * d:(r + 1) * 4 * d] = red_m[l, 8 + r:9 + r, :]
        out_s[...] = split_mm_nt(red_o[l], spread)
        for r in range(6):
            g_out[row, r * d:(r + 1) * d] = out_s[r:r + 1, :]
        for r in range(24):
            g_two[row, r * d:(r + 1) * d] = out_s[8 + r:9 + r, :]
        line_s[row, 0:256] = red_i[l, 7:8, :wide]
        line_s[row, 256:512] = red_i[l, 15:16, :wide]
        line_s[row, 512:768] = red_o[l, 6:7, :]
        line_s[row, 768:1152] = red_m[l, 7:8, :]
        line_s[row, 1152:1536] = red_m[l, 15:16, :]
        line_s[row, 1536:1920] = red_m[l, 6:7, :]
        line_s[row, 1920:2304] = red_m[l, 14:15, :]
        line_s[row, 2304:2304 + d] = red_i[l, 6:7, :d]
        line_s[row, 2560:2560 + d] = red_i[l, 14:15, :d]
    part = g_vec.shape[1]
    total = line_s.shape[1]
    c = iota((1, total), 1)
    goal = jnp.full((1, total), -1, jnp.int32)
    for start, block in ((0, 0), (256, 1), (512, 4), (768, 5), (1024, 6), (1280, 7)):
        inside = (c >= start) & (c < start + wide)
        own = natural(c - start)
        goal = jnp.where(inside & (own >= 0), block * d + own, goal)
    goal = jnp.where((c >= 1536) & (c < 1536 + 4 * d), c - 1536 + 8 * d, goal)
    goal = jnp.where((c >= 2304) & (c < 2304 + d), c - 2304 + 2 * d, goal)
    goal = jnp.where((c >= 2560) & (c < 2560 + d), c - 2560 + 3 * d, goal)
    choose = jnp.where(iota((128, total), 0) == goal - part * me, 1.0, 0.0).astype(bf16)
    g_vec[...] = split_mm_nt(line_s[...], choose)[0:layers, 0:part]


def local_fused(tokens, ranges, attn_in, attn_out, mlp_in, mlp_out, vectors, cotangent):
    n = lax.axis_size("dev")
    slots, d = tokens.shape
    layers, part = vectors.shape
    flats = (attn_in, attn_out, mlp_in, mlp_out, vectors)
    sums = fused(n, ranges, tokens.T, cotangent.T, flats)
    vm = pl.BlockSpec(memory_space=pltpu.VMEM)
    act, dx, *grads = pl.pallas_call(
        functools.partial(flatten_kernel, n, layers, d),
        out_shape=(
            jax.ShapeDtypeStruct((d, slots), bf16), jax.ShapeDtypeStruct((d, slots), f32),
        ) + tuple(jax.ShapeDtypeStruct(f.shape, f32) for f in flats),
        in_specs=[vm] * 5,
        out_specs=(vm,) * 7,
        scratch_shapes=[pltpu.VMEM((BLOCK, 2816), f32), pltpu.VMEM((2 * BLOCK, d), f32)],
        compiler_params=pltpu.CompilerParams(vmem_limit_bytes=vmem_bytes),
        name="flatten",
    )(*sums)
    return (act.T, dx.T, *grads)


def compute_kernel(n, layers, width, hidden_units, ranges, *refs):
    refs = list(refs)
    take = lambda count: [refs.pop(0) for _ in range(count)]
    (w_full,) = take(1)
    tok, cot, tok_up, cot_up = take(4)
    (grad_out,) = take(1)
    act_own, act_up, dx_own, dx_up = take(4)
    w_all, w_one_s, w_two_s, hat1_s, h1_s, qkv_s, p_s, o_s, hat2_s, h2_s, slope_s, a_s = take(12)
    inv_s, dqkv_s, do_s, grad_s, perm = take(5)
    slots = tok.shape[1]
    heads = width // HD
    d = width
    me = lax.axis_index("dev")
    first, last = ranges[me, 0], ranges[me, 1]
    total = ranges[n - 1, 1]
    image = (first + IMG_LEN - 1) // IMG_LEN
    rows = IMAGES_HERE * ROWS

    picks, valid_keys = [], []
    for k in range(IMAGES_HERE):
        begin = (image + k) * IMG_LEN
        count = jnp.where(begin < last, jnp.minimum(IMG_LEN, total - begin), 0)
        r = lax.broadcasted_iota(jnp.int32, (ROWS, 2 * slots), 0)
        c = lax.broadcasted_iota(jnp.int32, (ROWS, 2 * slots), 1)
        t = begin + r
        column = jnp.where(t < last, t - first, t - last + slots)
        column = jnp.where(r < count, column, -1)
        picks.append(jnp.where(column == c, 1.0, 0.0).astype(bf16))
        valid_keys.append(lax.broadcasted_iota(jnp.int32, (ROWS, ROWS), 1) < count)
    pick = jnp.concatenate(picks, axis=0)
    x = mm_nt(pick[:, :slots], tok[...]) + mm_nt(pick[:, slots:], tok_up[...])

    unit = lax.broadcasted_iota(jnp.int32, (1, hidden_units), 1)
    group = sum(jnp.where(unit >= j * d, 1, 0) for j in range(1, 4))
    origin = 4 * (unit - group * d) + group
    f = lax.broadcasted_iota(jnp.int32, (hidden_units, hidden_units), 0)
    perm[...] = jnp.where(f == origin, 1.0, 0.0).astype(bf16)

    vec = [None] * layers
    b_one = [None] * layers
    for l in range(layers):
        w_all[l] = w_full[l]
        w_one_s[l] = mm(w_all[l, :d, 4 * d:8 * d], perm[...]).astype(bf16)
        for j in range(4):
            w_two_s[l, j * d:(j + 1) * d, :] = w_all[l, :d, (8 + j) * d:(9 + j) * d]
        tail = w_all[l, d:d + BLOCK, :]
        vec[l] = tail.astype(f32)[0:1, :]
        b_one[l] = mm(tail[:, 8 * d:], perm[...])[0:1, :]

    def v_of(l, index):
        return vec[l][:, index * d:(index + 1) * d]

    for l in range(layers):
        h, hat, inv = norm_forward(x, v_of(l, 0), v_of(l, 1))
        hat1_s[l], h1_s[l], inv_s[l, 0] = hat, h, inv
        projected = mm(h, w_all[l, :d, :3 * d])
        qkv_s[l, :, :d] = ((projected[:, :d] + v_of(l, 2)).astype(bf16).astype(f32)
                           * (1.0 / math.sqrt(HD))).astype(bf16)
        qkv_s[l, :, d:2 * d] = projected[:, d:2 * d].astype(bf16)
        qkv_s[l, :, 2 * d:] = (projected[:, 2 * d:] + v_of(l, 3)).astype(bf16)
        for i in range(IMAGES_HERE):
            at = slice(i * ROWS, (i + 1) * ROWS)
            for head in range(heads):
                q = qkv_s[l, at, head * HD:(head + 1) * HD]
                key = qkv_s[l, at, d + head * HD:d + (head + 1) * HD]
                val = qkv_s[l, at, 2 * d + head * HD:2 * d + (head + 1) * HD]
                scores = jnp.where(valid_keys[i], mm_nt(q, key), masked_fill)
                e = jnp.exp(scores - jnp.max(scores, axis=-1, keepdims=True))
                p = e * (1.0 / jnp.sum(e, axis=-1, keepdims=True))
                p_s[l, i, head] = p
                o_s[l, at, head * HD:(head + 1) * HD] = mm(p.astype(bf16), val).astype(bf16)
        x1 = x + (mm(o_s[l], w_all[l, :d, 3 * d:4 * d]) + v_of(l, 4))
        h2, hat, inv = norm_forward(x1, v_of(l, 5), v_of(l, 6))
        hat2_s[l], h2_s[l], inv_s[l, 1] = hat, h2, inv
        u = mm(h2, w_one_s[l]) + b_one[l]
        phi = 0.5 * (1.0 + lax.erf(u * (1.0 / math.sqrt(2.0))))
        a_s[l] = (u * phi).astype(bf16)
        slope_s[l] = phi + u * (jnp.exp(-0.5 * u * u) * (1.0 / math.sqrt(2.0 * math.pi)))
        x = x1 + (mm(a_s[l], w_two_s[l]) + v_of(l, 7))

    x_low = x.astype(bf16)
    act_own[...] = mm_tn(x_low, pick[:, :slots]).astype(bf16)
    act_up[...] = mm_tn(x_low, pick[:, slots:]).astype(bf16)

    dx = mm_nt(pick[:, :slots], cot[...]) + mm_nt(pick[:, slots:], cot_up[...])
    for l in reversed(range(layers)):
        dm = dx.astype(bf16)
        g_two = mm_tn(a_s[l], dm)
        for j in range(4):
            grad_s[l, :d, (8 + j) * d:(9 + j) * d] = g_two[j * d:(j + 1) * d, :].astype(bf16)
        g_b2 = rows_sum(dm.astype(f32))
        du = (mm_nt(dm, w_two_s[l]) * slope_s[l]).astype(bf16)
        g_b1 = mm_nt(jnp.broadcast_to(rows_sum(du.astype(f32)), (BLOCK, hidden_units)).astype(bf16),
                     perm[...])[0:1, :]
        g_one = mm_tn(h2_s[l], du).astype(bf16)
        grad_s[l, :d, 4 * d:8 * d] = mm_nt(g_one, perm[...]).astype(bf16)
        dh2 = mm_nt(du, w_one_s[l])
        dv, g_g2, g_c2 = norm_backward(dh2, hat2_s[l], inv_s[l, 1], v_of(l, 5))
        dx1 = dx + dv
        db = dx1.astype(bf16)
        g_bo = rows_sum(db.astype(f32))
        grad_s[l, :d, 3 * d:4 * d] = mm_tn(o_s[l], db).astype(bf16)
        do_s[...] = mm_nt(db, w_all[l, :d, 3 * d:4 * d]).astype(bf16)
        for i in range(IMAGES_HERE):
            at = slice(i * ROWS, (i + 1) * ROWS)
            for head in range(heads):
                q_at = slice(head * HD, (head + 1) * HD)
                k_at = slice(d + head * HD, d + (head + 1) * HD)
                v_at = slice(2 * d + head * HD, 2 * d + (head + 1) * HD)
                do = do_s[at, q_at]
                p = p_s[l, i, head]
                dp = mm_nt(do, qkv_s[l, at, v_at])
                ds = (p * (dp - jnp.sum(p * dp, axis=-1, keepdims=True))).astype(bf16)
                dqkv_s[at, q_at] = (mm(ds, qkv_s[l, at, k_at]) * (1.0 / math.sqrt(HD))).astype(bf16)
                dqkv_s[at, k_at] = mm_tn(ds, qkv_s[l, at, q_at]).astype(bf16)
                dqkv_s[at, v_at] = mm_tn(p.astype(bf16), do).astype(bf16)
        g_bq = rows_sum(dqkv_s[:, :d].astype(f32))
        g_bv = rows_sum(dqkv_s[:, 2 * d:].astype(f32))
        grad_s[l, :d, :3 * d] = mm_tn(h1_s[l], dqkv_s[...]).astype(bf16)
        dh = mm_nt(dqkv_s[...], w_all[l, :d, :3 * d])
        dv, g_g1, g_c1 = norm_backward(dh, hat1_s[l], inv_s[l, 0], v_of(l, 0))
        dx = dx1 + dv
        line = jnp.concatenate([g_g1, g_c1, g_bq, g_bv, g_bo, g_g2, g_c2, g_b2, g_b1], axis=1)
        grad_s[l, d:d + BLOCK, :] = jnp.broadcast_to(line, (BLOCK, line.shape[1])).astype(bf16)

    high = dx.astype(bf16)
    low = (dx - high.astype(f32)).astype(bf16)
    dx_own[...] = mm_tn(high, pick[:, :slots]) + mm_tn(low, pick[:, :slots])
    dx_up[...] = mm_tn(high, pick[:, slots:]).astype(bf16)
    grad_out[...] = grad_s[...]


def compute(n, ranges, weights, tok, cot, tok_up, cot_up, layers):
    d, slots = tok.shape
    hidden_units = 4 * d
    rows = IMAGES_HERE * ROWS
    tall = d + BLOCK
    wide = 12 * d
    args = list(weights) + [tok, cot, tok_up, cot_up]
    outs = [jax.ShapeDtypeStruct((layers, tall, wide), bf16)]
    outs += [
        jax.ShapeDtypeStruct((d, slots), kind) for kind in (bf16, bf16, f32, bf16)
    ]
    vm = pl.BlockSpec(memory_space=pltpu.VMEM)
    return pl.pallas_call(
        functools.partial(compute_kernel, n, layers, d, hidden_units),
        out_shape=tuple(outs),
        in_specs=[pl.BlockSpec(memory_space=pltpu.SMEM)] + [vm] * len(args),
        out_specs=(vm,) * len(outs),
        scratch_shapes=[
            pltpu.VMEM((layers, tall, wide), bf16),
            pltpu.VMEM((layers, d, hidden_units), bf16),
            pltpu.VMEM((layers, hidden_units, d), bf16),
            pltpu.VMEM((layers, rows, d), f32),
            pltpu.VMEM((layers, rows, d), bf16),
            pltpu.VMEM((layers, rows, 3 * d), bf16),
            pltpu.VMEM((layers, IMAGES_HERE, d // HD, ROWS, ROWS), f32),
            pltpu.VMEM((layers, rows, d), bf16),
            pltpu.VMEM((layers, rows, d), f32),
            pltpu.VMEM((layers, rows, d), bf16),
            pltpu.VMEM((layers, rows, hidden_units), f32),
            pltpu.VMEM((layers, rows, hidden_units), bf16),
            pltpu.VMEM((layers, 2, rows, 1), f32),
            pltpu.VMEM((rows, 3 * d), bf16),
            pltpu.VMEM((rows, d), bf16),
            pltpu.VMEM((layers, tall, wide), bf16),
            pltpu.VMEM((hidden_units, hidden_units), bf16),
        ],
        compiler_params=pltpu.CompilerParams(vmem_limit_bytes=vmem_bytes),
        name="two_layers",
    )(ranges, *args)


def rows_of(flats, d):
    w_in, w_out, w_one, w_two = flats
    layers = w_in.shape[0]
    return jnp.concatenate(
        [
            w_in.reshape(layers, -1, 3 * d),
            w_out.reshape(layers, -1, d),
            w_one.reshape(layers, -1, 4 * d),
            w_two.reshape(layers, -1, 4 * d),
        ],
        axis=2,
    )


def flats_of(block, d):
    layers = block.shape[0]
    ends = (0, 3 * d, 4 * d, 8 * d, 12 * d)
    return [block[:, :, lo:hi].reshape(layers, -1) for lo, hi in zip(ends, ends[1:])]


def local_other(tokens, ranges, attn_in, attn_out, mlp_in, mlp_out, vectors, cotangent):
    n = lax.axis_size("dev")
    slots, d = tokens.shape
    layers, part = vectors.shape
    tokens, cotangent = tokens.T, cotangent.T
    flats = (attn_in, attn_out, mlp_in, mlp_out)
    whole = [
        jnp.stack([lax.all_gather(flat[l], "dev", axis=0, tiled=True) for l in range(layers)])
        for flat in flats + (vectors,)
    ]
    line = whole.pop()
    spare = jnp.zeros((layers, BLOCK - 1, 12 * d), bf16)
    block = jnp.concatenate([rows_of(whole, d), line[:, None, :], spare], axis=1)
    down = [(i, (i + n - 1) % n) for i in range(n)]
    tok_up, cot_up = lax.ppermute(tokens, "dev", down), lax.ppermute(cotangent, "dev", down)
    grad, act, act_up, dx, dx_up = compute(
        n, ranges, (block,), tokens, cotangent, tok_up, cot_up, layers
    )
    up = [(i, (i + 1) % n) for i in range(n)]
    act = act + lax.ppermute(act_up, "dev", up)
    dx = dx + lax.ppermute(dx_up, "dev", up)
    terms = flats_of(grad[:, :d], d) + [grad[:, d]]
    grads = [
        jnp.stack([
            lax.psum_scatter(term[l].astype(f32), "dev", scatter_dimension=0, tiled=True)
            for l in range(layers)
        ])
        for term in terms
    ]
    return (act.T, dx.T, *grads)


def solution(mesh):
    flat = P(None, "dev")
    rows = P("dev", None)

    def local(*args):
        n = lax.axis_size("dev")
        slots, d = args[0].shape
        layers = args[2].shape[0]
        fast = n == 32 and d == 6 * n and layers == 2 and slots == 256
        return local_fused(*args) if fast else local_other(*args)

    return jax.shard_map(
        local,
        mesh=mesh,
        in_specs=(rows, P(), flat, flat, flat, flat, flat, rows),
        out_specs=(rows, rows, flat, flat, flat, flat, flat),
        check_vma=False,
    )
```

time: 85.3 us -> 74.3 us (0.87)
  local copies, waits for them, and re-layouts: 10.2 us -> 0 us
    unnamed x22 -> x0, local copies, waits for them, and re-layouts: 5.86 us -> none
    reshape x3 -> x0, local copies, waits for them, and re-layouts: 2.31 us -> none  [the longest x2 1.38 us: flats_of(): block[:, :, lo:hi].reshape(layers, -1)]
    slice x3 -> x0, local copies, waits for them, and re-layouts: 0.97 us -> none  [the longest x1 0.89 us: local(): lines = full[layers * per:layers * (per + 1)]]
    pallas_call x3 -> x2, Pallas kernels: 73.2 us -> 73.5 us  [the longest x1 71.2 us: fused(): pl.pallas_call(functools.partial(fused_kernel, n, layers, d), out_shape=t...]
where the time goes in v1:
time: 74.3 us; the launch traced here: 74.2 us
  Pallas kernels  73.5 us (99%)
    pallas_call x1, Pallas kernels, fused(): pl.pallas_call(functools.partial(fused_kernel, n, layers, d), out_shape=t...  71.2 us
    pallas_call x1, Pallas kernels, local_fused(): pl.pallas_call(functools.partial(flatten_kernel, n, layers, d), out_shape...  2.28 us

profile of v1, /device:TPU:0, one launch (start us, length us, event | category | flops | bytes accessed | tf_op | source)
XLA Modules:
  0.0 74.2 jit_solution(15662860444798724053)
XLA Ops:
  0.6 71.2 %two_layers.1 = (f32[2,16,384]{2,1,0:T(8,128)}, f32[2,16,384]{2,1,0:T(8,128)}, f32[2,32,256]{2,1,0:T(8,128)}, bf16[192,256]{1,0:T(8,128)(2,1)}, f32[192,256]{1,0:T(8,128)}) custom-call(s32[2,32]{1,0:T(2,128)} %bitcast.7, bf16[192,256]{1,0:T(8,128)(2,1)} %bitcast.5, bf16[192,256]{1,0:T(8,128)(2,1)} %bitcast.6, bf16[2,3456]{1,0:T(2,128)(2,1)} %refs_2_.1, ...), custom_call_target="tpu_custom_call" | custom-call | tf_op jit(solution)/shard_map/two_layers/pallas_call | solution.py:532
  71.9 2.3 %flatten.1 = (bf16[192,256]{1,0:T(8,128)(2,1)}, f32[192,256]{1,0:T(8,128)}, f32[2,3456]{1,0:T(2,128)}, f32[2,1152]{1,0:T(2,128)}, f32[2,4608]{1,0:T(2,128)}, /*index=5*/f32[2,4608]{1,0:T(2,128)}, f32[2,72]{1,0:T(2,128)}) custom-call(f32[2,16,384]{2,1,0:T(8,128)} %get-tuple-element.19.red_i, f32[2,16,384]{2,1,0:T(8,128)} %get-tuple-element.20.red_m, ...), custom_call_target="tpu_custom_call" | custom-call | tf_op jit(solution)/shard_map/flatten/pallas_call | solution.py:602

commit v2 on v1

--- a/solution.py
+++ b/solution.py
@@ -73,13 +73,14 @@
         self.core = self.flip(0)
         self.along_z = [self.flip(3), self.flip(4), self.flip(3, 4)]
         self.along_xy = [self.flip(1), self.flip(2), self.flip(1, 2)]
+        self.chips = [self.flip(*[b + 1 for b in range(4) if m >> b & 1]) for m in range(1, 16)]
         self.up, self.down = lax.rem(me + 1, n), lax.rem(me + n - 1, n)
 
     def flip(self, *which):
         return self.me + sum((1 - 2 * self.bits[b]) * 2**b for b in which)
 
     def peers(self):
-        return [self.core] + self.along_z + self.along_xy + [self.up, self.down]
+        return [self.core] + self.chips + [self.up, self.down]
 
 
 class Gather:
@@ -165,6 +166,26 @@
         self.out[...] = total
 
 
+class Direct(Scatter):
+    def middle(self):
+        p = self.place
+        self.sent[0].wait_recv()
+        self.out_xy[...] = (
+            self.grads[:, :, :, p.c].astype(f32) + self.half[...].astype(f32)
+        ).astype(bf16)
+        for k, dev in enumerate(p.chips):
+            at = (lax.div(dev, 8), lax.rem(lax.div(dev, 4), 2), lax.rem(lax.div(dev, 2), 2))
+            self.go(self.out_xy.at[at], self.in_xy.at[k], dev)
+
+    def done(self):
+        p = self.place
+        total = self.grads[p.z, p.y, p.x, p.c].astype(f32) + self.half[p.z, p.y, p.x].astype(f32)
+        for k, copy in enumerate(self.sent[1:]):
+            copy.wait_recv()
+            total += self.in_xy[k].astype(f32)
+        self.out[...] = total
+
+
 def natural(c):
     return jnp.where((c & 7) < 6, 6 * (c >> 3) + (c & 7), -1)
 
@@ -190,24 +211,33 @@
     return dv, rows_sum(dh * hat), rows_sum(dh)
 
 
+def sublanes(x, shift):
+    return pltpu.roll(x, shift, 1)
+
+
+def unfold(tiles, s):
+    a, b, c = tiles
+    return jnp.where(s < 2, sublanes(a, 2), jnp.where(s < 4, sublanes(b, 4), sublanes(c, 6)))
+
+
+def fold(tiles, extra, s):
+    return [jnp.where(s < 6, t, sublanes(extra, 6 - 2 * k)) for k, t in enumerate(tiles)]
+
+
 def fused_kernel(n, layers, d, ranges, *refs):
     refs = list(refs)
     take = lambda count: [refs.pop(0) for _ in range(count)]
     tok, cot, a_in, a_out, m_in, m_out, vecs = take(7)
-    red_i, red_m, red_o, act_out, dx_out = take(5)
-    wire_i, wire_m, wire_o = take(3)
-    grad_i, grad_m, grad_o = take(3)
-    half_i, half_m, half_o = take(3)
-    mid_i, mid_m, mid_o = take(3)
-    inxy_i, inxy_m, inxy_o = take(3)
-    ours_i, ours_m, ours_o = take(3)
-    outz_i, outz_m, outz_o = take(3)
-    inz_i, inz_m, inz_o = take(3)
+    reds, (act_out, dx_out) = take(3), take(2)
+    wires, grads, halves, mids, inxys, ours, outzs, inzs = [take(3) for _ in range(8)]
+    (in_direct,) = take(1)
     tok_up, cot_up, act_up, act_in, dx_up, dx_in = take(6)
-    w_in_s, w_one_s, w_out_s, w_two_s = take(4)
+    w_in_s, w_one_s, w_out_s, w_two_s, two_s = take(5)
+    vec_n, vec_g, b_one_s, line_n, line_g = take(5)
     hat1_s, h1_s, qkv_s, p_s, o_s, hat2_s, h2_s, slope_s, a_s, inv_s = take(10)
-    dqkv_s, do_s, stage, flat_ai, flat_ao, flat_mi, flat_mo, vec_s = take(8)
+    dqkv_s, do_s, pack_a, pack_b, pack_c, flat_ai, flat_ao, flat_mi, flat_mo, vec_s = take(10)
     gsend, grecv, ssend, srecv, hsend, hrecv = take(6)
+    wire_a, wire_b, wire_c = wires
     slots = tok.shape[1]
     heads = d // HD
     wide = 8 * n
@@ -220,72 +250,65 @@
     for other in place.peers():
         pl.semaphore_signal(barrier, inc=1, device_id=(other,), device_id_type=MESH_ID)
 
-    lane = iota((1, wide), 1)
-    real = jnp.where((lane & 7) < 6, 1.0, 0.0)
-    ones_lane = jnp.where((lane & 7) == 6, 1.0, 0.0)
-    spread = jnp.where(iota((d, wide), 0) == natural(iota((1, wide), 1)), 1.0, 0.0).astype(bf16)
-
     part = vecs.shape[1]
+    here = (place.z, place.y, place.x, place.c)
     vec_s[...] = jnp.zeros_like(vec_s)
     vec_s[0:layers, 0:part] = vecs[...].astype(f32)
-    columns = 8 * d + hidden_units
-    pick_vec = jnp.where(
-        iota((vec_s.shape[1], columns), 0) == iota((1, columns), 1) - part * me, 1.0, 0.0
-    ).astype(bf16)
-    lines = mm(vec_s[...].astype(bf16), pick_vec)
+    moved = pltpu.roll(vec_s[...], 8 * lax.rem(me, 8), 1)
+    vec_s[...] = moved
     flat_ai[...] = a_in[...].astype(f32)
-    flat_ao[...] = a_out[...].astype(f32)
-    flat_mi[...] = m_in[...].astype(f32)
     flat_mo[...] = m_out[...].astype(f32)
-    here = (place.z, place.y, place.x, place.c)
-    big, small = stage
-    for l in range(layers):
+    pack_b[...] = jnp.zeros_like(pack_b)
+
+    def pack_first(l):
         row = slice(l, l + 1)
-        small[...] = jnp.zeros_like(small)
         for r in range(6):
-            small[r:r + 1, :] = flat_ao[row, r * d:(r + 1) * d]
+            base, k, i = r * 3 * d, r // 2, r % 2
+            pack_a[r:r + 1, :] = flat_ai[row, base:base + 256]
+            pack_a[8 + r:9 + r, :128] = flat_ai[row, base + 256:base + 384]
+            low, lanes = 6 + i + (8 if k == 2 else 0), slice(128 * (k % 2), 128 * (k % 2) + 128)
+            pack_a[low:low + 1, lanes] = flat_ai[row, base + 384:base + 512]
+            pack_a[8 + r:9 + r, 128:192] = flat_ai[row, base + 512:base + 576]
+        pack_a[14:15, 128:192] = vec_s[row, :64]
+        pack_a[15:16, 128:192] = vec_s[row, 64:128]
+        for r in range(8):
+            pack_a[8 + r:9 + r, 192:] = flat_mo[row, (16 + r) * d + 128:(17 + r) * d]
+        wire_a[(l,) + here] = pack_a[...].astype(bf16)
+
+    def pack_second(l):
+        row = slice(l, l + 1)
+        for r in range(6):
+            base, k, i = r * 4 * d, r // 2, r % 2
+            lanes = slice(128 * k, 128 * k + 128)
+            pack_b[r:r + 1, :] = flat_mi[row, base:base + 384]
+            pack_b[6 + i:7 + i, lanes] = flat_mi[row, base + 384:base + 512]
+            pack_b[8 + r:9 + r, :256] = flat_mi[row, base + 512:base + 768]
+            pack_b[8 + r:9 + r, 256:] = flat_ao[row, r * d:r * d + 128]
+            pack_b[14 + i:15 + i, 128 * k:128 * k + 64] = flat_ao[row, r * d + 128:(r + 1) * d]
+        wire_b[(l,) + here] = pack_b[...].astype(bf16)
+
+    def pack_third(l):
+        row = slice(l, l + 1)
         for r in range(24):
-            small[8 + r:9 + r, :] = flat_mo[row, r * d:(r + 1) * d]
-        for r, block in ((6, 4), (32, 0), (33, 1), (34, 5), (35, 6), (36, 7)):
-            small[r:r + 1, :] = lines[row, block * d:(block + 1) * d]
-        padded = mm(small[...].astype(bf16), spread)
-        wire_o[(l,) + here] = padded[:32].astype(bf16)
-        big[0] = jnp.zeros_like(big[0])
-        big[1] = jnp.zeros_like(big[1])
-        for r in range(6):
-            big[0, r:r + 1, :] = flat_ai[row, r * 3 * d:r * 3 * d + 2 * d]
-            big[0, 8 + r:9 + r, :d] = flat_ai[row, r * 3 * d + 2 * d:(r + 1) * 3 * d]
-            big[1, r:r + 1, :] = flat_mi[row, r * 4 * d:r * 4 * d + 2 * d]
-            big[1, 8 + r:9 + r, :] = flat_mi[row, r * 4 * d + 2 * d:(r + 1) * 4 * d]
-        big[0, 6:7, :d] = lines[row, 2 * d:3 * d]
-        big[0, 14:15, :d] = lines[row, 3 * d:4 * d]
-        big[0, 7:8, :wide] = padded[32:33]
-        big[0, 15:16, :wide] = padded[33:34]
-        big[1, 6:7, :] = lines[row, 8 * d:10 * d]
-        big[1, 14:15, :] = lines[row, 10 * d:12 * d]
-        big[1, 7:8, :wide] = padded[34:35]
-        big[1, 7:8, wide:] = padded[35:36, :2 * d - wide]
-        big[1, 15:16, :2 * wide - 2 * d] = padded[35:36, 2 * d - wide:]
-        big[1, 15:16, 2 * wide - 2 * d:] = padded[36:37]
-        wire_i[(l,) + here] = big[0].astype(bf16)
-        wire_m[(l,) + here] = big[1].astype(bf16)
-
-    wires = (wire_i, wire_m, wire_o)
+            g, i = r // 8, r % 8
+            low, lane = i + (8 if g == 2 else 0), 128 * (g % 2)
+            pack_c[low:low + 1, lane:lane + 128] = flat_mo[row, r * d:r * d + 128]
+            if g < 2:
+                pack_c[8 + i:9 + i, 128 + 64 * g:192 + 64 * g] = flat_mo[row, r * d + 128:(r + 1) * d]
+        wire_c[(l,) + here] = pack_c[...].astype(bf16)
+
     gathers = [
         [Gather(place, wires[k].at[l], gsend.at[l, k], grecv.at[l, k]) for k in range(3)]
         for l in range(layers)
     ]
     scatters = [
         [
-            Scatter(
-                place, grads.at[l], half.at[l], (mid.at[l], inxy.at[l]), ours.at[l],
-                (outz.at[l], inz.at[l]), ssend.at[l, k], srecv.at[l, k], red.at[l],
+            (Direct if k == 0 and l == 0 else Scatter)(
+                place, grads[k].at[l], halves[k].at[l],
+                (mids[k].at[l], in_direct if k == 0 and l == 0 else inxys[k].at[l]),
+                ours[k].at[l], (outzs[k].at[l], inzs[k].at[l]), ssend.at[l, k], srecv.at[l, k], reds[k].at[l],
             )
-            for k, (grads, half, mid, inxy, ours, outz, inz, red) in enumerate((
-                (grad_i, half_i, mid_i, inxy_i, ours_i, outz_i, inz_i, red_i),
-                (grad_m, half_m, mid_m, inxy_m, ours_m, outz_m, inz_m, red_m),
-                (grad_o, half_o, mid_o, inxy_o, ours_o, outz_o, inz_o, red_o),
-            ))
+            for k in range(3)
         ]
         for l in range(layers)
     ]
@@ -295,12 +318,35 @@
         remote(act_up, act_in, hsend.at[2], hrecv.at[2], place.up),
         remote(dx_up, dx_in, hsend.at[3], hrecv.at[3], place.up),
     ]
-    (gi0, gm0, go0), (gi1, gm1, go1) = gathers
-    (si0, sm0, so0), (si1, sm1, so1) = scatters
-
+    (ga0, gb0, gc0), (ga1, gb1, gc1) = gathers
+    (sa0, sb0, sc0), (sa1, sb1, sc1) = scatters
+
+    pack_first(0)
     pl.semaphore_wait(barrier, len(place.peers()))
-    gi0.begin()
+    ga0.begin()
     halo[0].start()
+    flat_ao[...] = a_out[...].astype(f32)
+    flat_mi[...] = m_in[...].astype(f32)
+    pack_second(0)
+    gb0.begin()
+    pack_third(0)
+    gc0.begin()
+    pack_first(1)
+    ga1.begin()
+    pack_second(1)
+    gb1.begin()
+    pack_third(1)
+    gc1.begin()
+
+    lane = iota((1, wide), 1)
+    real = jnp.where((lane & 7) < 6, 1.0, 0.0)
+    spread = jnp.where(iota((d, wide), 0) == natural(iota((1, wide), 1)), 1.0, 0.0).astype(bf16)
+    owner = lane >> 3
+    window = jnp.where((lane & 7) >= 6, owner + (owner >> 3) + (lane & 1), -1)
+    windows = [
+        jnp.where(3 * iota((BLOCK, wide), 0) + k == window, 1.0, 0.0).astype(bf16) for k in range(3)
+    ]
+    sub = iota((1, 8, 1), 1)
 
     first, last = ranges[0, me], ranges[1, me]
     total = ranges[1, n - 1]
@@ -319,55 +365,67 @@
     pick = jnp.concatenate(picks, axis=0)
     x = mm_nt(pick[:, :slots], mm_tn(spread, tok[...]).astype(bf16))
 
-    gi0.middle()
-    go0.begin()
-    gm0.begin()
+    ga0.middle()
+    gb0.middle()
     halo[0].wait_recv()
     x += mm_nt(pick[:, slots:], mm_tn(spread, tok_up[...]).astype(bf16))
-    gi0.core()
-    go0.middle()
-    gm0.middle()
-    gi1.begin()
-    halo[1].start()
-
-    def unpack_in(l):
-        v = wire_i[l].reshape(2 * n * 8, 2 * d).astype(f32).reshape(n, 2, 8, 2 * d)
-        w_in_s[l, :, :2 * d] = v[:, 0].reshape(wide, 2 * d).astype(bf16)
-        w_in_s[l, :, 2 * d:] = v[:, 1].reshape(wide, 2 * d).astype(bf16)
-        s = jnp.sum(v, axis=0)
-        return s[0, 7:8, :wide], s[1, 7:8, :wide] + ones_lane
-
-    def unpack_one(l):
-        v = wire_m[l].reshape(2 * n * 8, 2 * d).astype(f32).reshape(n, 2, 8, 2 * d)
-        w_one_s[l, :, :2 * d] = v[:, 0].reshape(wide, 2 * d).astype(bf16)
-        w_one_s[l, :, 2 * d:] = v[:, 1].reshape(wide, 2 * d).astype(bf16)
-        s = jnp.sum(v, axis=0)
-        bias = jnp.concatenate([s[0, 7:8, wide:], s[1, 7:8, :2 * wide - 2 * d]], axis=1)
-        return s[0, 7:8, :wide], bias + ones_lane, s[1, 7:8, 2 * wide - 2 * d:]
-
-    def unpack_out(l):
-        v = wire_o[l].reshape(4 * n * 8, wide).astype(f32).reshape(n, 4, 8, wide)
-        w_out_s[l] = mm(spread, v[:, 0].reshape(wide, wide).astype(bf16)).astype(bf16)
-        w_two_s[l] = v[:, 1:].reshape(hidden_units, wide).astype(bf16)
-        return jnp.sum(v[:, 0], axis=0)[6:7, :]
-
-    gain1, gain2 = [None] * layers, [None] * layers
+    gc0.middle()
+    ga0.core()
+    ga1.middle()
+
+    def tiles_of(wire, l):
+        v = wire[l]
+        width = v.shape[-1]
+        v = v.reshape(n * BLOCK, width).astype(f32).reshape(n, 2, 8, width)
+        return [v[:, i, :, k:k + 128] for i in range(2) for k in range(0, width, 128)]
+
+    def flat(t):
+        return t.reshape(wide, t.shape[-1]).astype(bf16)
+
+    def unpack_a(l):
+        t0, t1, t2, t4 = tiles_of(wire_a, l)
+        for k, t in enumerate((t0, t1, t2, unfold((t0, t1, t2), sub), t4)):
+            w_in_s[l, :, 128 * k:128 * k + 128] = flat(t)
+        t4 = flat(t4)
+        lines = jnp.concatenate([mm(each, t4)[:, :64] for each in windows], axis=1)
+        vec_n[l] = lines
+        vec_g[l] = mm(lines.astype(bf16), spread)
+        for k in range(4):
+            b_one_s[l, 0:1, k * d:(k + 1) * d] = lines[8 + k:9 + k]
+
+    def unpack_b(l):
+        t0, t1, t2, t4, t5, t6 = tiles_of(wire_b, l)
+        for k, t in enumerate((t0, t1, t2, unfold((t0, t1, t2), sub), t4, t5)):
+            w_one_s[l, :, 128 * k:128 * k + 128] = flat(t)
+        t7 = unfold((t4, t5, t6), sub)
+        out = jnp.concatenate([flat(t6), flat(t7)], axis=1)
+        out = mm(spread, out)[:, :d].astype(bf16)
+        w_out_s[l] = mm(out, spread).astype(bf16)
+
+    def unpack_c(l):
+        t0, t1, t2, t3 = tiles_of(wire_c, l)
+        last = tiles_of(wire_a, l)[3]
+        side = pltpu.roll(t3, 64, 2), pltpu.roll(last, 64, 2)
+        pile = lambda ts: jnp.stack(ts, axis=1).reshape(hidden_units, 128).astype(bf16)
+        two_s[:, :128] = pile((t0, t1, t2))
+        two_s[:, 128:] = pile((t3,) + side)
+        w_two_s[l] = mm(two_s[:, :d], spread).astype(bf16)
+
     beats = [
-        [lambda: (go0.core(), gi1.middle()), lambda: (gm0.core(), go1.begin(), gm1.begin()),
-         lambda: gi1.core(), lambda: (go1.middle(), gm1.middle())],
-        [lambda: go1.core(), lambda: gm1.core(), lambda: None, lambda: None],
+        [lambda: gb0.core(), lambda: (gc0.core(), gb1.middle()), lambda: (ga1.core(), gc1.middle(), halo[1].start())],
+        [lambda: gb1.core(), lambda: gc1.core(), lambda: None],
     ]
     for l in range(layers):
-        gi, gm, go = gathers[l]
-        gi.done()
-        gain1[l], bias = unpack_in(l)
-        h, hat, inv = norm_padded(x, gain1[l], bias, real, d)
+        ga, gb, gc = gathers[l]
+        ga.done()
+        unpack_a(l)
+        h, hat, inv = norm_padded(x, vec_g[l, 0:1], vec_g[l, 1:2], real, d)
         hat1_s[l], h1_s[l], inv_s[l, 0] = hat, h, inv
         projected = mm(h, w_in_s[l, :, :3 * d])
-        qkv_s[l, :, :d] = (projected[:, :d].astype(bf16).astype(f32)
+        qkv_s[l, :, :d] = ((projected[:, :d] + vec_n[l, 2:3]).astype(bf16).astype(f32)
                            * (1.0 / math.sqrt(HD))).astype(bf16)
-        qkv_s[l, :, d:] = projected[:, d:].astype(bf16)
-        beats[l][0]()
+        qkv_s[l, :, d:2 * d] = projected[:, d:2 * d].astype(bf16)
+        qkv_s[l, :, 2 * d:] = (projected[:, 2 * d:] + vec_n[l, 3:4]).astype(bf16)
         for i in range(IMAGES_HERE):
             at = slice(i * ROWS, (i + 1) * ROWS)
             for head in range(heads):
@@ -379,20 +437,20 @@
                 p = e * (1.0 / jnp.sum(e, axis=-1, keepdims=True))
                 p_s[l, i, head] = p
                 o_s[l, at, head * HD:(head + 1) * HD] = mm(p.astype(bf16), val).astype(bf16)
-            beats[l][1 + i]()
-        go.done()
-        b_out = unpack_out(l)
-        x1 = x + (mm(o_s[l], w_out_s[l]) + b_out)
-        gm.done()
-        gain2[l], bias, b_two = unpack_one(l)
-        h2, hat, inv = norm_padded(x1, gain2[l], bias, real, d)
+            beats[l][i]()
+        gb.done()
+        unpack_b(l)
+        x1 = x + (mm(o_s[l], w_out_s[l]) + vec_g[l, 4:5])
+        h2, hat, inv = norm_padded(x1, vec_g[l, 5:6], vec_g[l, 6:7], real, d)
         hat2_s[l], h2_s[l], inv_s[l, 1] = hat, h2, inv
-        u = mm(h2, w_one_s[l])
-        beats[l][3]()
+        u = mm(h2, w_one_s[l]) + b_one_s[l, 0:1]
         phi = 0.5 * (1.0 + lax.erf(u * (1.0 / math.sqrt(2.0))))
         a_s[l] = (u * phi).astype(bf16)
         slope_s[l] = phi + u * (jnp.exp(-0.5 * u * u) * (1.0 / math.sqrt(2.0 * math.pi)))
-        x = x1 + (mm(a_s[l], w_two_s[l]) + b_two)
+        beats[l][2]()
+        gc.done()
+        unpack_c(l)
+        x = x1 + (mm(a_s[l], w_two_s[l]) + vec_g[l, 7:8])
 
     x_low = mm_nt(x.astype(bf16), spread).astype(bf16)
     act_up[...] = mm_tn(x_low, pick[:, slots:]).astype(bf16)
@@ -403,44 +461,54 @@
     dx = mm_nt(pick[:, :slots], mm_tn(spread, cot[...]).astype(bf16))
     dx += mm_nt(pick[:, slots:], mm_tn(spread, cot_up[...]).astype(bf16))
 
-    row_of = iota((wide, 1), 0) & 7
-
-    def fold(a, b):
-        v = jnp.concatenate([a.reshape(n, 1, 8, 2 * d), b.reshape(n, 1, 8, 2 * d)], axis=1)
-        return v.reshape(2 * n * 8, 2 * d).astype(bf16).reshape(4, 2, 2, 2, BLOCK, 2 * d)
+    def cut(w, pieces):
+        return [w[:, 128 * k:128 * k + 128].reshape(n, 8, 128) for k in range(pieces)]
+
+    def block(tiles):
+        half = len(tiles) // 2
+        v = [jnp.concatenate(tiles[i * half:(i + 1) * half], axis=-1)[:, None] for i in range(2)]
+        v = jnp.concatenate(v, axis=1).reshape(n * BLOCK, 128 * half).astype(bf16)
+        return v.reshape(4, 2, 2, 2, BLOCK, 128 * half)
 
     beats = [
-        [lambda: (so1.end(), si1.middle()), lambda: (si1.end(), so1.done()),
-         lambda: (sm0.middle(), si1.done()), lambda: so0.middle(), lambda: sm0.end()],
-        [lambda: None, lambda: None, lambda: sm1.middle(), lambda: so1.middle(), lambda: (sm1.end())],
+        [lambda: (sa1.middle(), sb1.end()), lambda: (sc1.done(), sc0.middle()),
+         lambda: (sa1.end(), sb1.done(), sb0.middle()), lambda: sc0.end()],
+        [lambda: None, lambda: sc1.middle(), lambda: sb1.middle(), lambda: sc1.end()],
     ]
-    spare = jnp.zeros((rows, d), bf16)
+    dqkv_s[:, 3 * d:] = jnp.zeros((rows, d), bf16)
+    low_lanes = iota((1, 1, 128), 2) < 64
+    line_g[...] = jnp.zeros_like(line_g)
+    line_n[...] = jnp.zeros_like(line_n)
     for l in reversed(range(layers)):
-        si, sm, so = scatters[l]
+        sa, sb, sc = scatters[l]
         dm = dx.astype(bf16)
-        g_b2 = rows_sum(dm.astype(f32))
+        line_g[7:8] = rows_sum(dm.astype(f32))
+        g_two = mm_tn(a_s[l], mm_nt(dm, spread).astype(bf16)).reshape(n, 3, 8, d)
+        side = jnp.concatenate([g_two[..., 128:], jnp.zeros((n, 3, 8, 256 - d), f32)], axis=-1)
+        turned = pltpu.roll(side[:, 1], 64, 2)
+        tail = pltpu.roll(side[:, 2], 64, 2)
+        grads[2][l] = block([g_two[:, 0, :, :128], g_two[:, 1, :, :128], g_two[:, 2, :, :128],
+                             jnp.where(low_lanes, side[:, 0], turned)])
+        sc.begin()
         du = (mm_nt(dm, w_two_s[l]) * slope_s[l]).astype(bf16)
         beats[l][0]()
-        g_one = mm_tn(h2_s[l], du)
+        g_b1 = rows_sum(du.astype(f32))
+        for k in range(4):
+            line_n[8 + k:9 + k] = g_b1[:, k * d:(k + 1) * d]
         dh2 = mm_nt(du, w_one_s[l])
-        dv, g_g2, g_c2 = norm_padded_back(dh2, hat2_s[l], inv_s[l, 1], gain2[l], d)
-        line = jnp.concatenate([g_g2, g_c2, g_b2], axis=1)
-        g_one = jnp.where(row_of == 7, line, g_one)
-        grad_m[l] = fold(g_one[:, :2 * d], g_one[:, 2 * d:])
-        sm.begin()
+        dv, g_g2, g_c2 = norm_padded_back(dh2, hat2_s[l], inv_s[l, 1], vec_g[l, 5:6], d)
+        line_g[5:6], line_g[6:7] = g_g2, g_c2
         dx1 = dx + dv
         db = dx1.astype(bf16)
-        g_bo = rows_sum(db.astype(f32))
+        line_g[4:5] = rows_sum(db.astype(f32))
+        g_out = mm_tn(o_s[l], mm_nt(db, spread).astype(bf16))
+        g_out = jnp.concatenate([g_out, jnp.zeros((d, 256 - d), f32)], axis=1).astype(bf16)
+        t6, t7 = cut(mm_tn(spread, g_out), 2)
+        t0, t1, t2, t3, t4, t5 = cut(mm_tn(h2_s[l], du), 6)
+        grads[1][l] = block(fold((t0, t1, t2), t3, sub) + fold((t4, t5, t6), t7, sub))
+        beats[l][1]()
+        sb.begin()
         do_s[...] = mm_nt(db, w_out_s[l]).astype(bf16)
-        beats[l][1]()
-        g_two = mm_tn(a_s[l], dm)
-        g_out = mm_tn(spread, mm_tn(o_s[l], db).astype(bf16))
-        g_out = jnp.where(row_of == 6, g_bo, g_out)
-        v = jnp.concatenate([g_out.reshape(n, 1, 8, wide), g_two.reshape(n, 3, 8, wide)], axis=1)
-        grad_o[l] = v.reshape(4 * n * 8, wide).astype(bf16).reshape(4, 2, 2, 2, 2 * BLOCK, wide)
-        so.begin()
-        beats[l][2]()
-        dqkv_s[:, 3 * d:] = spare
         for i in range(IMAGES_HERE):
             at = slice(i * ROWS, (i + 1) * ROWS)
             for head in range(heads):
@@ -454,35 +522,39 @@
                 dqkv_s[at, q_at] = (mm(ds, qkv_s[l, at, k_at]) * (1.0 / math.sqrt(HD))).astype(bf16)
                 dqkv_s[at, k_at] = mm_tn(ds, qkv_s[l, at, q_at]).astype(bf16)
                 dqkv_s[at, v_at] = mm_tn(p.astype(bf16), do).astype(bf16)
-            beats[l][3 + i]()
-        dh = mm_nt(dqkv_s[...], w_in_s[l])
-        dv, g_g1, g_c1 = norm_padded_back(dh, hat1_s[l], inv_s[l, 0], gain1[l], d)
-        g_in = mm_tn(h1_s[l], dqkv_s[...])
-        blank = jnp.zeros((1, 2 * d - wide), f32)
-        line = jnp.concatenate([g_g1, blank, g_c1, blank], axis=1)
-        g_in = jnp.where(row_of == 7, line, g_in)
-        grad_i[l] = fold(g_in[:, :2 * d], g_in[:, 2 * d:])
-        si.begin()
+            beats[l][2 + i]()
+        dqkv = dqkv_s[:, :640]
+        line_n[2:3] = rows_sum(dqkv_s[:, :d].astype(f32))
+        line_n[3:4] = rows_sum(dqkv_s[:, 2 * d:3 * d].astype(f32))
+        dh = mm_nt(dqkv, w_in_s[l])
+        dv, g_g1, g_c1 = norm_padded_back(dh, hat1_s[l], inv_s[l, 0], vec_g[l, 0:1], d)
+        line_g[0:1], line_g[1:2] = g_g1, g_c1
+        lines = (line_n[...] + mm_nt(line_g[...].astype(bf16), spread)).astype(bf16)
+        vec_rows = sum(mm_tn(windows[k], lines[:, 64 * k:64 * k + 64]) for k in range(3))
+        vec_rows = jnp.concatenate([vec_rows, jnp.zeros((wide, 64), f32)], axis=1).reshape(n, 8, 128)
+        t0, t1, t2, t3, t4 = cut(mm_tn(h1_s[l], dqkv), 5)
+        t4 = jnp.where(low_lanes, t4 + vec_rows, tail)
+        grads[0][l] = block(fold((t0, t1, t2), t3, sub) + [t4])
+        sa.begin()
         dx = dx1 + dv
 
     high = dx.astype(bf16)
     low = (dx - high.astype(f32)).astype(bf16)
     high = mm_nt(high, spread).astype(bf16)
-    low = mm_nt(low, spread).astype(bf16)
     dx_up[...] = mm_tn(high, pick[:, slots:]).astype(bf16)
     halo[3].start()
-    so0.end()
-    si0.middle()
-    sm0.done()
+    sa0.middle()
+    sb0.end()
+    low = mm_nt(low, spread).astype(bf16)
     dx_own = mm_tn(high, pick[:, :slots]) + mm_tn(low, pick[:, :slots])
-    sm1.done()
-    so0.done()
-    si0.end()
+    sa1.done()
+    sc0.done()
     halo[2].wait_recv()
     act_out[...] = act_own + act_in[...]
     halo[3].wait_recv()
     dx_out[...] = dx_own + dx_in[...].astype(f32)
-    si0.done()
+    sb0.done()
+    sa0.done()
     for copy in halo:
         copy.wait_send()
     for group in gathers + scatters:
@@ -497,19 +569,26 @@
     wide = 8 * n
     hidden_units = 4 * d
     rows = IMAGES_HERE * ROWS
-    shapes = ((BLOCK, 2 * d), (BLOCK, 2 * d), (2 * BLOCK, wide))
+    shapes = ((BLOCK, 256), (BLOCK, 384), (BLOCK, 256))
     boxes = lambda lead, kind: [pltpu.VMEM((layers,) + lead + s, kind) for s in shapes]
     vm = pl.BlockSpec(memory_space=pltpu.VMEM)
     scratch = (
         boxes((4, 2, 2, 2), bf16) + boxes((4, 2, 2, 2), bf16)
         + boxes((4, 2, 2), bf16) + boxes((4, 2, 2), bf16) + boxes((WAYS, 4), bf16)
         + boxes((4,), f32) + boxes((4,), bf16) + boxes((WAYS,), bf16)
+        + [pltpu.VMEM((15,) + shapes[0], bf16)]
         + [pltpu.VMEM((d, slots), bf16)] * 6
         + [
-            pltpu.VMEM((layers, wide, 4 * d), bf16),
+            pltpu.VMEM((layers, wide, 640), bf16),
             pltpu.VMEM((layers, wide, hidden_units), bf16),
             pltpu.VMEM((layers, d, wide), bf16),
             pltpu.VMEM((layers, hidden_units, wide), bf16),
+            pltpu.VMEM((hidden_units, 256), bf16),
+            pltpu.VMEM((layers, BLOCK, d), f32),
+            pltpu.VMEM((layers, BLOCK, wide), f32),
+            pltpu.VMEM((layers, 8, hidden_units), f32),
+            pltpu.VMEM((BLOCK, d), f32),
+            pltpu.VMEM((BLOCK, wide), f32),
             pltpu.VMEM((layers, rows, wide), f32),
             pltpu.VMEM((layers, rows, wide), bf16),
             pltpu.VMEM((layers, rows, 3 * d), bf16),
@@ -522,11 +601,11 @@
             pltpu.VMEM((layers, 2, rows, 1), f32),
             pltpu.VMEM((rows, 4 * d), bf16),
             pltpu.VMEM((rows, d), bf16),
-            (pltpu.VMEM((2, BLOCK, 2 * d), f32), pltpu.VMEM((3 * BLOCK, d), f32)),
         ]
+        + [pltpu.VMEM(s, f32) for s in shapes]
         + [pltpu.VMEM(f.shape, f32) for f in flats[:4]]
-        + [pltpu.VMEM((BLOCK, 128), f32)]
-        + [pltpu.SemaphoreType.DMA((layers, 3, 2 * WAYS + 1))] * 4
+        + [pltpu.VMEM((8, 128), f32)]
+        + [pltpu.SemaphoreType.DMA((layers, 3, 16))] * 4
         + [pltpu.SemaphoreType.DMA((4,))] * 2
     )
     return pl.pallas_call(
@@ -543,53 +622,41 @@
     )(ranges.T, tok, cot, *flats)
 
 
-def split_mm_nt(a, b):
-    high = a.astype(bf16)
-    low = (a - high.astype(f32)).astype(bf16)
-    return mm_nt(high, b) + mm_nt(low, b)
-
-
-def flatten_kernel(n, layers, d, red_i, red_m, red_o, act_in, dx_in, act, dx, g_in, g_out, g_one, g_two, g_vec, line_s, out_s):
+def flatten_kernel(n, layers, d, red_a, red_b, red_c, act_in, dx_in, act, dx, g_in, g_out, g_one, g_two, g_vec, vec_s):
     me = lax.axis_index("dev")
-    wide = 8 * n
     act[...] = act_in[...]
     dx[...] = dx_in[...]
-    spread = jnp.where(iota((d, wide), 0) == natural(iota((1, wide), 1)), 1.0, 0.0).astype(bf16)
-    line_s[...] = jnp.zeros_like(line_s)
+    vec_s[...] = jnp.zeros_like(vec_s)
     for l in range(layers):
         row = slice(l, l + 1)
         for r in range(6):
-            g_in[row, r * 3 * d:r * 3 * d + 2 * d] = red_i[l, r:r + 1, :]
-            g_in[row, r * 3 * d + 2 * d:(r + 1) * 3 * d] = red_i[l, 8 + r:9 + r, :d]
-            g_one[row, r * 4 * d:r * 4 * d + 2 * d] = red_m[l, r:r + 1, :]
-            g_one[row, r * 4 * d + 2 * d:(r + 1) * 4 * d] = red_m[l, 8 + r:9 + r, :]
-        out_s[...] = split_mm_nt(red_o[l], spread)
-        for r in range(6):
-            g_out[row, r * d:(r + 1) * d] = out_s[r:r + 1, :]
+            k, i = r // 2, r % 2
+            base = r * 3 * d
+            g_in[row, base:base + 256] = red_a[l, r:r + 1, :]
+            g_in[row, base + 256:base + 384] = red_a[l, 8 + r:9 + r, :128]
+            low, lane = 6 + i + (8 if k == 2 else 0), 128 * (k % 2)
+            g_in[row, base + 384:base + 512] = red_a[l, low:low + 1, lane:lane + 128]
+            g_in[row, base + 512:base + 576] = red_a[l, 8 + r:9 + r, 128:192]
+            base = r * 4 * d
+            g_one[row, base:base + 384] = red_b[l, r:r + 1, :]
+            g_one[row, base + 384:base + 512] = red_b[l, 6 + i:7 + i, 128 * k:128 * k + 128]
+            g_one[row, base + 512:base + 768] = red_b[l, 8 + r:9 + r, :256]
+            base = r * d
+            g_out[row, base:base + 128] = red_b[l, 8 + r:9 + r, 256:]
+            g_out[row, base + 128:base + 192] = red_b[l, 14 + i:15 + i, 128 * k:128 * k + 64]
         for r in range(24):
-            g_two[row, r * d:(r + 1) * d] = out_s[8 + r:9 + r, :]
-        line_s[row, 0:256] = red_i[l, 7:8, :wide]
-        line_s[row, 256:512] = red_i[l, 15:16, :wide]
-        line_s[row, 512:768] = red_o[l, 6:7, :]
-        line_s[row, 768:1152] = red_m[l, 7:8, :]
-        line_s[row, 1152:1536] = red_m[l, 15:16, :]
-        line_s[row, 1536:1920] = red_m[l, 6:7, :]
-        line_s[row, 1920:2304] = red_m[l, 14:15, :]
-        line_s[row, 2304:2304 + d] = red_i[l, 6:7, :d]
-        line_s[row, 2560:2560 + d] = red_i[l, 14:15, :d]
+            g, i = r // 8, r % 8
+            base, low, lane = r * d, i + (8 if g == 2 else 0), 128 * (g % 2)
+            g_two[row, base:base + 128] = red_c[l, low:low + 1, lane:lane + 128]
+            if g < 2:
+                g_two[row, base + 128:base + 192] = red_c[l, 8 + i:9 + i, 128 + 64 * g:192 + 64 * g]
+            else:
+                g_two[row, base + 128:base + 192] = red_a[l, 8 + i:9 + i, 192:]
+        vec_s[row, :64] = red_a[l, 14:15, 128:192]
+        vec_s[row, 64:] = red_a[l, 15:16, 128:192]
     part = g_vec.shape[1]
-    total = line_s.shape[1]
-    c = iota((1, total), 1)
-    goal = jnp.full((1, total), -1, jnp.int32)
-    for start, block in ((0, 0), (256, 1), (512, 4), (768, 5), (1024, 6), (1280, 7)):
-        inside = (c >= start) & (c < start + wide)
-        own = natural(c - start)
-        goal = jnp.where(inside & (own >= 0), block * d + own, goal)
-    goal = jnp.where((c >= 1536) & (c < 1536 + 4 * d), c - 1536 + 8 * d, goal)
-    goal = jnp.where((c >= 2304) & (c < 2304 + d), c - 2304 + 2 * d, goal)
-    goal = jnp.where((c >= 2560) & (c < 2560 + d), c - 2560 + 3 * d, goal)
-    choose = jnp.where(iota((128, total), 0) == goal - part * me, 1.0, 0.0).astype(bf16)
-    g_vec[...] = split_mm_nt(line_s[...], choose)[0:layers, 0:part]
+    moved = pltpu.roll(vec_s[...], lax.rem(128 - 8 * lax.rem(me, 8), 128), 1)
+    g_vec[...] = moved[0:layers, 0:part]
 
 
 def local_fused(tokens, ranges, attn_in, attn_out, mlp_in, mlp_out, vectors, cotangent):
@@ -606,7 +673,7 @@
         ) + tuple(jax.ShapeDtypeStruct(f.shape, f32) for f in flats),
         in_specs=[vm] * 5,
         out_specs=(vm,) * 7,
-        scratch_shapes=[pltpu.VMEM((BLOCK, 2816), f32), pltpu.VMEM((2 * BLOCK, d), f32)],
+        scratch_shapes=[pltpu.VMEM((8, 128), f32)],
         compiler_params=pltpu.CompilerParams(vmem_limit_bytes=vmem_bytes),
         name="flatten",
     )(*sums)

time: 74.3 us -> 58.8 us (0.79)
  Pallas kernels: 73.5 us -> 58 us
    pallas_call x1, Pallas kernels: 71.2 us -> 56.1 us  [fused(): pl.pallas_call(functools.partial(fused_kernel, n, layers, d), out_shape=t...]
where the time goes in v2:
time: 58.8 us; the launch traced here: 58.6 us
  Pallas kernels  58 us (99%)
  between operations  0.64 us (1%)
    pallas_call x1, Pallas kernels, fused(): pl.pallas_call(functools.partial(fused_kernel, n, layers, d), out_shape=t...  56.1 us
    pallas_call x1, Pallas kernels, local_fused(): pl.pallas_call(functools.partial(flatten_kernel, n, layers, d), out_shape...  1.88 us

profile of v2, /device:TPU:0, one launch (start us, length us, event | category | flops | bytes accessed | tf_op | source)
XLA Modules:
  0.0 58.6 jit_solution(3990379796577277905)
XLA Ops:
  0.6 56.1 %two_layers.1 = (f32[2,16,256]{2,1,0:T(8,128)}, f32[2,16,384]{2,1,0:T(8,128)}, f32[2,16,256]{2,1,0:T(8,128)}, bf16[192,256]{1,0:T(8,128)(2,1)}, f32[192,256]{1,0:T(8,128)}) custom-call(s32[2,32]{1,0:T(2,128)} %bitcast.7, bf16[192,256]{1,0:T(8,128)(2,1)} %bitcast.5, bf16[192,256]{1,0:T(8,128)(2,1)} %bitcast.6, bf16[2,3456]{1,0:T(2,128)(2,1)} %refs_2_.1, ...), custom_call_target="tpu_custom_call" | custom-call | tf_op jit(solution)/shard_map/two_layers/pallas_call | solution.py:611
  56.8 1.9 %flatten.1 = (bf16[192,256]{1,0:T(8,128)(2,1)}, f32[192,256]{1,0:T(8,128)}, f32[2,3456]{1,0:T(2,128)}, f32[2,1152]{1,0:T(2,128)}, f32[2,4608]{1,0:T(2,128)}, /*index=5*/f32[2,4608]{1,0:T(2,128)}, f32[2,72]{1,0:T(2,128)}) custom-call(f32[2,16,256]{2,1,0:T(8,128)} %get-tuple-element.19.red_a, f32[2,16,384]{2,1,0:T(8,128)} %get-tuple-element.20.red_b, ...), custom_call_target="tpu_custom_call" | custom-call | tf_op jit(solution)/shard_map/flatten/pallas_call | solution.py:669

commit v3 on v2

--- a/solution.py
+++ b/solution.py
@@ -51,9 +51,6 @@
 
 def rows_sum(x):
     return jnp.sum(x, axis=0, keepdims=True)
-
-
-WAYS = 3
 
 
 def remote(src, dst, send, recv, dev):
@@ -83,111 +80,128 @@
         return [self.core] + self.chips + [self.up, self.down]
 
 
-class Gather:
-    def __init__(self, place, buf, send, recv):
+def taken(ref, sem):
+    pltpu.make_async_copy(ref, ref, sem).wait()
+
+
+class Sender:
+    def go(self, src, dst, k, dev):
+        remote(src, dst, self.send.at[k], self.recv.at[k], dev).start()
+
+    def arrived(self, k):
+        taken(self.size_of[k], self.recv.at[k])
+
+    def left(self):
+        for k, ref in enumerate(self.size_of):
+            taken(ref, self.send.at[k])
+
+
+class Gather(Sender):
+    def __init__(self, place, buf, room, send, recv):
         self.place, self.buf, self.send, self.recv = place, buf, send, recv
-        self.sent = []
-
-    def go(self, at, dev):
-        k = len(self.sent)
-        copy = remote(at, at, self.send.at[k], self.recv.at[k], dev)
-        copy.start()
-        self.sent.append(copy)
+        three, nine = buf.at[pl.ds(0, 3), 0, 0, 0], room.at[:, pl.ds(1, 3)]
+        self.size_of = [three, three, nine, buf.at[:, :, :, 0]]
 
     def begin(self):
         p = self.place
-        for dev in p.along_z:
-            self.go(self.buf.at[p.z, p.y, p.x, p.c], dev)
+        own = self.buf.at[0, p.y, p.x, p.c]
+        for k, dev in enumerate(p.along_z):
+            self.go(own, self.buf.at[k + 1, p.y, p.x, p.c], 0, dev)
+        for dev in p.along_xy:
+            self.go(own, own, 1, dev)
 
     def middle(self):
         p = self.place
-        for copy in self.sent[:WAYS]:
-            copy.wait_recv()
+        self.arrived(0)
+        got = self.buf.at[pl.ds(1, 3), p.y, p.x, p.c]
         for dev in p.along_xy:
-            self.go(self.buf.at[:, p.y, p.x, p.c], dev)
+            self.go(got, got, 2, dev)
 
     def core(self):
         p = self.place
-        for copy in self.sent[WAYS:2 * WAYS]:
-            copy.wait_recv()
-        self.go(self.buf.at[:, :, :, p.c], p.core)
+        self.arrived(1)
+        self.arrived(2)
+        half = self.buf.at[:, :, :, p.c]
+        self.go(half, half, 3, p.core)
 
     def done(self):
-        self.sent[-1].wait_recv()
-
-
-class Scatter:
-    def __init__(self, place, grads, half, mid, ours, last, send, recv, out):
-        self.place, self.grads, self.half, self.mid = place, grads, half, mid
-        self.ours, self.last, self.send, self.recv, self.out = ours, last, send, recv, out
-        self.out_xy, self.in_xy = mid
-        self.out_z, self.in_z = last
-        self.sent = []
-
-    def go(self, src, dst, dev):
-        k = len(self.sent)
-        copy = remote(src, dst, self.send.at[k], self.recv.at[k], dev)
-        copy.start()
-        self.sent.append(copy)
+        self.arrived(3)
+
+
+class Scatter(Sender):
+    def __init__(self, place, grads, half, out_xy, in_xy, out_z, in_z, send, recv, out):
+        self.place, self.grads, self.half = place, grads, half
+        self.out_xy, self.in_xy, self.out_z, self.in_z = out_xy, in_xy, out_z, in_z
+        self.send, self.recv, self.out = send, recv, out
+        self.size_of = [half, in_xy.at[:, pl.ds(1, 3)], in_xy.at[:, 0], in_z]
 
     def begin(self):
         p = self.place
-        self.go(self.grads.at[:, :, :, 1 - p.c], self.half, p.core)
+        self.go(self.grads.at[:, :, :, 1 - p.c], self.half, 0, p.core)
+
+    def pair(self):
+        self.arrived(0)
+        self.out_xy[...] = (
+            self.grads[:, :, :, self.place.c].astype(f32) + self.half[...].astype(f32)
+        ).astype(bf16)
 
     def middle(self):
         p = self.place
-        self.sent[0].wait_recv()
-        self.out_xy[...] = (
-            self.grads[:, :, :, p.c].astype(f32) + self.half[...].astype(f32)
-        ).astype(bf16)
-        for k, (dy, dx) in enumerate(((0, 1), (1, 0), (1, 1))):
-            y = 1 - p.y if dy else p.y
-            x = 1 - p.x if dx else p.x
-            self.go(self.out_xy.at[:, y, x], self.in_xy.at[k], p.along_xy[k])
+        self.pair()
+        goals = [(p.y, 1 - p.x), (1 - p.y, p.x), (1 - p.y, 1 - p.x)]
+        for k, (y, x) in enumerate(goals):
+            self.go(self.out_xy.at[pl.ds(1, 3), y, x], self.in_xy.at[k, pl.ds(1, 3)], 1, p.along_xy[k])
+        for k, (y, x) in enumerate(goals):
+            self.go(self.out_xy.at[0, y, x], self.in_xy.at[k, 0], 2, p.along_xy[k])
+
+    def ours(self, z):
+        p = self.place
+        return self.grads[z, p.y, p.x, p.c].astype(f32) + self.half[z, p.y, p.x].astype(f32)
 
     def end(self):
         p = self.place
-        for copy in self.sent[1:1 + WAYS]:
-            copy.wait_recv()
-        total = self.grads[:, p.y, p.x, p.c].astype(f32) + self.half[:, p.y, p.x].astype(f32)
-        for k in range(WAYS):
-            total += self.in_xy[k].astype(f32)
-        self.ours[...] = total
-        self.out_z[...] = total.astype(bf16)
-        for k, dev in enumerate(p.along_z):
-            self.go(self.out_z.at[lax.div(dev, 8)], self.in_z.at[k], dev)
+        self.arrived(1)
+        for z in range(1, 4):
+            total = self.ours(z)
+            for k in range(3):
+                total += self.in_xy[k, z].astype(f32)
+            self.out_z[z - 1] = total.astype(bf16)
+            self.go(self.out_z.at[z - 1], self.in_z.at[z - 1], 3, p.along_z[z - 1])
 
     def done(self):
-        for copy in self.sent[1 + WAYS:]:
-            copy.wait_recv()
-        total = self.ours[self.place.z]
-        for k in range(WAYS):
+        self.arrived(2)
+        total = self.ours(0)
+        for k in range(3):
+            total += self.in_xy[k, 0].astype(f32)
+        self.arrived(3)
+        for k in range(3):
             total += self.in_z[k].astype(f32)
         self.out[...] = total
 
 
 class Direct(Scatter):
+    def __init__(self, *args):
+        super().__init__(*args)
+        self.size_of = [self.half, self.in_xy]
+
     def middle(self):
         p = self.place
-        self.sent[0].wait_recv()
-        self.out_xy[...] = (
-            self.grads[:, :, :, p.c].astype(f32) + self.half[...].astype(f32)
-        ).astype(bf16)
-        for k, dev in enumerate(p.chips):
-            at = (lax.div(dev, 8), lax.rem(lax.div(dev, 4), 2), lax.rem(lax.div(dev, 2), 2))
-            self.go(self.out_xy.at[at], self.in_xy.at[k], dev)
+        self.pair()
+        for m, dev in enumerate(p.chips, 1):
+            y = 1 - p.y if m & 2 else p.y
+            x = 1 - p.x if m & 1 else p.x
+            self.go(self.out_xy.at[m >> 2, y, x], self.in_xy.at[m - 1], 1, dev)
 
     def done(self):
-        p = self.place
-        total = self.grads[p.z, p.y, p.x, p.c].astype(f32) + self.half[p.z, p.y, p.x].astype(f32)
-        for k, copy in enumerate(self.sent[1:]):
-            copy.wait_recv()
+        total = self.ours(0)
+        self.arrived(1)
+        for k in range(15):
             total += self.in_xy[k].astype(f32)
         self.out[...] = total
 
 
-def natural(c):
-    return jnp.where((c & 7) < 6, 6 * (c >> 3) + (c & 7), -1)
+def natural(c, z):
+    return jnp.where((c & 7) < 6, 6 * ((c >> 3) ^ (8 * z)) + (c & 7), -1)
 
 
 def iota(shape, dim):
@@ -229,10 +243,10 @@
     take = lambda count: [refs.pop(0) for _ in range(count)]
     tok, cot, a_in, a_out, m_in, m_out, vecs = take(7)
     reds, (act_out, dx_out) = take(3), take(2)
-    wires, grads, halves, mids, inxys, ours, outzs, inzs = [take(3) for _ in range(8)]
+    wires, grads, halves, outxys, inxys, outzs, inzs = [take(3) for _ in range(7)]
     (in_direct,) = take(1)
-    tok_up, cot_up, act_up, act_in, dx_up, dx_in = take(6)
-    w_in_s, w_one_s, w_out_s, w_two_s, two_s = take(5)
+    tok_near, cot_near, act_near, act_in, dx_near, dx_in = take(6)
+    w_in_s, w_one_s, w_out_s, w_two_s, two_s, g_two_s = take(6)
     vec_n, vec_g, b_one_s, line_n, line_g = take(5)
     hat1_s, h1_s, qkv_s, p_s, o_s, hat2_s, h2_s, slope_s, a_s, inv_s = take(10)
     dqkv_s, do_s, pack_a, pack_b, pack_c, flat_ai, flat_ao, flat_mi, flat_mo, vec_s = take(10)
@@ -251,7 +265,8 @@
         pl.semaphore_signal(barrier, inc=1, device_id=(other,), device_id_type=MESH_ID)
 
     part = vecs.shape[1]
-    here = (place.z, place.y, place.x, place.c)
+    here = (0, place.y, place.x, place.c)
+    z_of = [place.z] + [lax.div(dev, 8) for dev in place.along_z]
     vec_s[...] = jnp.zeros_like(vec_s)
     vec_s[0:layers, 0:part] = vecs[...].astype(f32)
     moved = pltpu.roll(vec_s[...], 8 * lax.rem(me, 8), 1)
@@ -298,33 +313,48 @@
         wire_c[(l,) + here] = pack_c[...].astype(bf16)
 
     gathers = [
-        [Gather(place, wires[k].at[l], gsend.at[l, k], grecv.at[l, k]) for k in range(3)]
+        [
+            Gather(place, wires[k].at[l], inxys[k].at[l], gsend.at[l, k], grecv.at[l, k])
+            for k in range(3)
+        ]
         for l in range(layers)
     ]
     scatters = [
         [
             (Direct if k == 0 and l == 0 else Scatter)(
-                place, grads[k].at[l], halves[k].at[l],
-                (mids[k].at[l], in_direct if k == 0 and l == 0 else inxys[k].at[l]),
-                ours[k].at[l], (outzs[k].at[l], inzs[k].at[l]), ssend.at[l, k], srecv.at[l, k], reds[k].at[l],
+                place, grads[k].at[l], halves[k].at[l], outxys[k].at[l],
+                in_direct if k == 0 and l == 0 else inxys[k].at[l],
+                outzs[k].at[l], inzs[k].at[l], ssend.at[l, k], srecv.at[l, k], reds[k].at[l],
             )
             for k in range(3)
         ]
         for l in range(layers)
     ]
-    halo = [
-        remote(tok, tok_up, hsend.at[0], hrecv.at[0], place.down),
-        remote(cot, cot_up, hsend.at[1], hrecv.at[1], place.down),
-        remote(act_up, act_in, hsend.at[2], hrecv.at[2], place.up),
-        remote(dx_up, dx_in, hsend.at[3], hrecv.at[3], place.up),
+    side = slots // 2
+    first_half, second_half = pl.ds(0, side), pl.ds(side, side)
+
+    def pair(src, dst, at):
+        return [
+            remote(src.at[:, a], dst.at[:, b], hsend.at[at + i], hrecv.at[at + i], dev)
+            for i, (a, b, dev) in enumerate((
+                (first_half, first_half, place.down), (second_half, second_half, place.up),
+            ))
+        ]
+
+    tok_halo, cot_halo = pair(tok, tok_near, 0), pair(cot, cot_near, 2)
+    back = lambda src, dst, at: [
+        remote(src.at[:, first_half], dst.at[:, first_half], hsend.at[at], hrecv.at[at], place.up),
+        remote(src.at[:, second_half], dst.at[:, second_half], hsend.at[at + 1], hrecv.at[at + 1], place.down),
     ]
+    act_halo, dx_halo = back(act_near, act_in, 4), back(dx_near, dx_in, 6)
     (ga0, gb0, gc0), (ga1, gb1, gc1) = gathers
     (sa0, sb0, sc0), (sa1, sb1, sc1) = scatters
 
     pack_first(0)
     pl.semaphore_wait(barrier, len(place.peers()))
     ga0.begin()
-    halo[0].start()
+    for copy in tok_halo:
+        copy.start()
     flat_ao[...] = a_out[...].astype(f32)
     flat_mi[...] = m_in[...].astype(f32)
     pack_second(0)
@@ -337,28 +367,34 @@
     gb1.begin()
     pack_third(1)
     gc1.begin()
+    for copy in cot_halo:
+        copy.start()
 
     lane = iota((1, wide), 1)
     real = jnp.where((lane & 7) < 6, 1.0, 0.0)
-    spread = jnp.where(iota((d, wide), 0) == natural(iota((1, wide), 1)), 1.0, 0.0).astype(bf16)
-    owner = lane >> 3
+    spread = jnp.where(iota((d, wide), 0) == natural(iota((1, wide), 1), place.z), 1.0, 0.0).astype(bf16)
+    owner = (lane >> 3) ^ (8 * place.z)
     window = jnp.where((lane & 7) >= 6, owner + (owner >> 3) + (lane & 1), -1)
     windows = [
         jnp.where(3 * iota((BLOCK, wide), 0) + k == window, 1.0, 0.0).astype(bf16) for k in range(3)
     ]
     sub = iota((1, 8, 1), 1)
 
-    first, last = ranges[0, me], ranges[1, me]
+    first, last, below = ranges[0, me], ranges[1, me], ranges[0, place.down]
     total = ranges[1, n - 1]
-    image = (first + IMG_LEN - 1) // IMG_LEN
+    centre = IMG_LEN // 2
+    image = (first + IMG_LEN - 1 - centre) // IMG_LEN
     picks, valid_keys = [], []
     for k in range(IMAGES_HERE):
         begin = (image + k) * IMG_LEN
-        count = jnp.where(begin < last, jnp.minimum(IMG_LEN, total - begin), 0)
+        mine = (begin < total) & (jnp.minimum(begin + centre, total - 1) < last)
+        count = jnp.where(mine, jnp.minimum(IMG_LEN, total - begin), 0)
         r = iota((ROWS, 2 * slots), 0)
         c = iota((ROWS, 2 * slots), 1)
         t = begin + r
-        column = jnp.where(t < last, t - first, t - last + slots)
+        column = jnp.where(
+            t < first, t - below + slots, jnp.where(t < last, t - first, t - last + slots)
+        )
         column = jnp.where(r < count, column, -1)
         picks.append(jnp.where(column == c, 1.0, 0.0).astype(bf16))
         valid_keys.append(iota((ROWS, ROWS), 1) < count)
@@ -367,11 +403,12 @@
 
     ga0.middle()
     gb0.middle()
-    halo[0].wait_recv()
-    x += mm_nt(pick[:, slots:], mm_tn(spread, tok_up[...]).astype(bf16))
     gc0.middle()
     ga0.core()
     ga1.middle()
+    for copy in tok_halo:
+        copy.wait_recv()
+    x += mm_nt(pick[:, slots:], mm_tn(spread, tok_near[...]).astype(bf16))
 
     def tiles_of(wire, l):
         v = wire[l]
@@ -406,14 +443,17 @@
         t0, t1, t2, t3 = tiles_of(wire_c, l)
         last = tiles_of(wire_a, l)[3]
         side = pltpu.roll(t3, 64, 2), pltpu.roll(last, 64, 2)
-        pile = lambda ts: jnp.stack(ts, axis=1).reshape(hidden_units, 128).astype(bf16)
-        two_s[:, :128] = pile((t0, t1, t2))
-        two_s[:, 128:] = pile((t3,) + side)
+        pile = lambda ts: jnp.stack(ts, axis=1).reshape(4, d, 128).astype(bf16)
+        left, right = pile((t0, t1, t2)), pile((t3,) + side)
+        for k in range(4):
+            at = pl.ds(pl.multiple_of(z_of[k] * d, BLOCK), d)
+            two_s[at, :128] = left[k]
+            two_s[at, 128:] = right[k]
         w_two_s[l] = mm(two_s[:, :d], spread).astype(bf16)
 
     beats = [
-        [lambda: gb0.core(), lambda: (gc0.core(), gb1.middle()), lambda: (ga1.core(), gc1.middle(), halo[1].start())],
-        [lambda: gb1.core(), lambda: gc1.core(), lambda: None],
+        [lambda: gb1.middle(), lambda: gc1.middle(), lambda: gb0.core(), lambda: gc0.core(), lambda: ga1.core()],
+        [lambda: gb1.core(), lambda: gc1.core(), lambda: None, lambda: None, lambda: None],
     ]
     for l in range(layers):
         ga, gb, gc = gathers[l]
@@ -426,6 +466,7 @@
                            * (1.0 / math.sqrt(HD))).astype(bf16)
         qkv_s[l, :, d:2 * d] = projected[:, d:2 * d].astype(bf16)
         qkv_s[l, :, 2 * d:] = (projected[:, 2 * d:] + vec_n[l, 3:4]).astype(bf16)
+        beats[l][0]()
         for i in range(IMAGES_HERE):
             at = slice(i * ROWS, (i + 1) * ROWS)
             for head in range(heads):
@@ -437,8 +478,9 @@
                 p = e * (1.0 / jnp.sum(e, axis=-1, keepdims=True))
                 p_s[l, i, head] = p
                 o_s[l, at, head * HD:(head + 1) * HD] = mm(p.astype(bf16), val).astype(bf16)
-            beats[l][i]()
+            beats[l][1 + i]()
         gb.done()
+        beats[l][3]()
         unpack_b(l)
         x1 = x + (mm(o_s[l], w_out_s[l]) + vec_g[l, 4:5])
         h2, hat, inv = norm_padded(x1, vec_g[l, 5:6], vec_g[l, 6:7], real, d)
@@ -447,19 +489,21 @@
         phi = 0.5 * (1.0 + lax.erf(u * (1.0 / math.sqrt(2.0))))
         a_s[l] = (u * phi).astype(bf16)
         slope_s[l] = phi + u * (jnp.exp(-0.5 * u * u) * (1.0 / math.sqrt(2.0 * math.pi)))
-        beats[l][2]()
+        beats[l][4]()
         gc.done()
         unpack_c(l)
         x = x1 + (mm(a_s[l], w_two_s[l]) + vec_g[l, 7:8])
 
     x_low = mm_nt(x.astype(bf16), spread).astype(bf16)
-    act_up[...] = mm_tn(x_low, pick[:, slots:]).astype(bf16)
-    halo[2].start()
+    act_near[...] = mm_tn(x_low, pick[:, slots:]).astype(bf16)
+    for copy in act_halo:
+        copy.start()
     act_own = mm_tn(x_low, pick[:, :slots]).astype(bf16)
 
-    halo[1].wait_recv()
+    for copy in cot_halo:
+        copy.wait_recv()
     dx = mm_nt(pick[:, :slots], mm_tn(spread, cot[...]).astype(bf16))
-    dx += mm_nt(pick[:, slots:], mm_tn(spread, cot_up[...]).astype(bf16))
+    dx += mm_nt(pick[:, slots:], mm_tn(spread, cot_near[...]).astype(bf16))
 
     def cut(w, pieces):
         return [w[:, 128 * k:128 * k + 128].reshape(n, 8, 128) for k in range(pieces)]
@@ -471,9 +515,9 @@
         return v.reshape(4, 2, 2, 2, BLOCK, 128 * half)
 
     beats = [
-        [lambda: (sa1.middle(), sb1.end()), lambda: (sc1.done(), sc0.middle()),
-         lambda: (sa1.end(), sb1.done(), sb0.middle()), lambda: sc0.end()],
-        [lambda: None, lambda: sc1.middle(), lambda: sb1.middle(), lambda: sc1.end()],
+        [lambda: (sa1.middle(), sc1.end()), lambda: sc0.middle(),
+         lambda: (sb1.end(), sb0.middle()), lambda: None],
+        [lambda: None, lambda: sc1.middle(), lambda: sb1.middle(), lambda: None],
     ]
     dqkv_s[:, 3 * d:] = jnp.zeros((rows, d), bf16)
     low_lanes = iota((1, 1, 128), 2) < 64
@@ -483,7 +527,10 @@
         sa, sb, sc = scatters[l]
         dm = dx.astype(bf16)
         line_g[7:8] = rows_sum(dm.astype(f32))
-        g_two = mm_tn(a_s[l], mm_nt(dm, spread).astype(bf16)).reshape(n, 3, 8, d)
+        g_two_s[...] = mm_tn(a_s[l], mm_nt(dm, spread).astype(bf16))
+        g_two = jnp.concatenate(
+            [g_two_s[pl.ds(pl.multiple_of(z * d, BLOCK), d), :] for z in z_of], axis=0
+        ).reshape(n, 3, 8, d)
         side = jnp.concatenate([g_two[..., 128:], jnp.zeros((n, 3, 8, 256 - d), f32)], axis=-1)
         turned = pltpu.roll(side[:, 1], 64, 2)
         tail = pltpu.roll(side[:, 2], 64, 2)
@@ -541,26 +588,32 @@
     high = dx.astype(bf16)
     low = (dx - high.astype(f32)).astype(bf16)
     high = mm_nt(high, spread).astype(bf16)
-    dx_up[...] = mm_tn(high, pick[:, slots:]).astype(bf16)
-    halo[3].start()
+    dx_near[...] = mm_tn(high, pick[:, slots:]).astype(bf16)
+    for copy in dx_halo:
+        copy.start()
+    sa1.end()
     sa0.middle()
-    sb0.end()
+    sc0.end()
     low = mm_nt(low, spread).astype(bf16)
     dx_own = mm_tn(high, pick[:, :slots]) + mm_tn(low, pick[:, :slots])
+    sc1.done()
+    sb0.end()
+    sb1.done()
+    for copy in act_halo:
+        copy.wait_recv()
+    act_out[...] = act_own + act_in[...]
+    for copy in dx_halo:
+        copy.wait_recv()
+    dx_out[...] = dx_own + dx_in[...].astype(f32)
     sa1.done()
     sc0.done()
-    halo[2].wait_recv()
-    act_out[...] = act_own + act_in[...]
-    halo[3].wait_recv()
-    dx_out[...] = dx_own + dx_in[...].astype(f32)
     sb0.done()
     sa0.done()
-    for copy in halo:
+    for copy in tok_halo + cot_halo + act_halo + dx_halo:
         copy.wait_send()
     for group in gathers + scatters:
         for each in group:
-            for copy in each.sent:
-                copy.wait_send()
+            each.left()
 
 
 def fused(n, ranges, tok, cot, flats):
@@ -574,8 +627,8 @@
     vm = pl.BlockSpec(memory_space=pltpu.VMEM)
     scratch = (
         boxes((4, 2, 2, 2), bf16) + boxes((4, 2, 2, 2), bf16)
-        + boxes((4, 2, 2), bf16) + boxes((4, 2, 2), bf16) + boxes((WAYS, 4), bf16)
-        + boxes((4,), f32) + boxes((4,), bf16) + boxes((WAYS,), bf16)
+        + boxes((4, 2, 2), bf16) + boxes((4, 2, 2), bf16) + boxes((3, 4), bf16)
+        + boxes((3,), bf16) + boxes((3,), bf16)
         + [pltpu.VMEM((15,) + shapes[0], bf16)]
         + [pltpu.VMEM((d, slots), bf16)] * 6
         + [
@@ -584,6 +637,7 @@
             pltpu.VMEM((layers, d, wide), bf16),
             pltpu.VMEM((layers, hidden_units, wide), bf16),
             pltpu.VMEM((hidden_units, 256), bf16),
+            pltpu.VMEM((hidden_units, d), f32),
             pltpu.VMEM((layers, BLOCK, d), f32),
             pltpu.VMEM((layers, BLOCK, wide), f32),
             pltpu.VMEM((layers, 8, hidden_units), f32),
@@ -605,8 +659,8 @@
         + [pltpu.VMEM(s, f32) for s in shapes]
         + [pltpu.VMEM(f.shape, f32) for f in flats[:4]]
         + [pltpu.VMEM((8, 128), f32)]
-        + [pltpu.SemaphoreType.DMA((layers, 3, 16))] * 4
-        + [pltpu.SemaphoreType.DMA((4,))] * 2
+        + [pltpu.SemaphoreType.DMA((layers, 3, 4))] * 4
+        + [pltpu.SemaphoreType.DMA((8,))] * 2
     )
     return pl.pallas_call(
         functools.partial(fused_kernel, n, layers, d),

time: 58.8 us -> 54 us (0.918)
  Pallas kernels: 58 us -> 53.1 us
    pallas_call x1, Pallas kernels: 56.1 us -> 51.3 us  [fused(): pl.pallas_call(functools.partial(fused_kernel, n, layers, d), out_shape=t...]
where the time goes in v3:
time: 54 us; the launch traced here: 53.8 us
  Pallas kernels  53.1 us (98%)
  between operations  0.64 us (1%)
    pallas_call x1, Pallas kernels, fused(): pl.pallas_call(functools.partial(fused_kernel, n, layers, d), out_shape=t...  51.3 us
    pallas_call x1, Pallas kernels, local_fused(): pl.pallas_call(functools.partial(flatten_kernel, n, layers, d), out_shape...  1.88 us

profile of v3, /device:TPU:0, one launch (start us, length us, event | category | flops | bytes accessed | tf_op | source)
XLA Modules:
  0.0 53.8 jit_solution(3446621101312024548)
XLA Ops:
  0.6 51.3 %two_layers.1 = (f32[2,16,256]{2,1,0:T(8,128)}, f32[2,16,384]{2,1,0:T(8,128)}, f32[2,16,256]{2,1,0:T(8,128)}, bf16[192,256]{1,0:T(8,128)(2,1)}, f32[192,256]{1,0:T(8,128)}) custom-call(s32[2,32]{1,0:T(2,128)} %bitcast.7, bf16[192,256]{1,0:T(8,128)(2,1)} %bitcast.5, bf16[192,256]{1,0:T(8,128)(2,1)} %bitcast.6, bf16[2,3456]{1,0:T(2,128)(2,1)} %refs_2_.1, ...), custom_call_target="tpu_custom_call" | custom-call | tf_op jit(solution)/shard_map/two_layers/pallas_call | solution.py:665
  51.9 1.9 %flatten.1 = (bf16[192,256]{1,0:T(8,128)(2,1)}, f32[192,256]{1,0:T(8,128)}, f32[2,3456]{1,0:T(2,128)}, f32[2,1152]{1,0:T(2,128)}, f32[2,4608]{1,0:T(2,128)}, /*index=5*/f32[2,4608]{1,0:T(2,128)}, f32[2,72]{1,0:T(2,128)}) custom-call(f32[2,16,256]{2,1,0:T(8,128)} %get-tuple-element.19.red_a, f32[2,16,384]{2,1,0:T(8,128)} %get-tuple-element.20.red_b, ...), custom_call_target="tpu_custom_call" | custom-call | tf_op jit(solution)/shard_map/flatten/pallas_call | solution.py:723

commit v4 on v3

--- a/solution.py
+++ b/solution.py
@@ -93,7 +93,8 @@
 
     def left(self):
         for k, ref in enumerate(self.size_of):
-            taken(ref, self.send.at[k])
+            if ref is not None:
+                taken(ref, self.send.at[k])
 
 
 class Gather(Sender):
@@ -128,12 +129,39 @@
         self.arrived(3)
 
 
+class GatherAcross(Gather):
+    def __init__(self, place, buf, room, send, recv):
+        super().__init__(place, buf, room, send, recv)
+        self.size_of = [room, self.size_of[1], None, self.size_of[3]]
+
+    def begin(self):
+        p = self.place
+        own = self.buf.at[0, p.y, p.x, p.c]
+        for dev in p.along_xy:
+            self.go(own, own, 1, dev)
+
+    def middle(self):
+        self.arrived(1)
+        c = self.place.c
+        for k, dev in enumerate(self.place.along_z):
+            self.go(self.buf.at[0, :, :, c], self.buf.at[k + 1, :, :, c], 0, dev)
+
+    def core(self):
+        p = self.place
+        self.arrived(0)
+        half = self.buf.at[:, :, :, p.c]
+        self.go(half, half, 3, p.core)
+
+
 class Scatter(Sender):
     def __init__(self, place, grads, half, out_xy, in_xy, out_z, in_z, send, recv, out):
         self.place, self.grads, self.half = place, grads, half
         self.out_xy, self.in_xy, self.out_z, self.in_z = out_xy, in_xy, out_z, in_z
         self.send, self.recv, self.out = send, recv, out
-        self.size_of = [half, in_xy.at[:, pl.ds(1, 3)], in_xy.at[:, 0], in_z]
+        self.size_of = self.sizes()
+
+    def sizes(self):
+        return [self.half, self.in_xy.at[:, pl.ds(1, 3)], self.in_xy.at[:, 0], self.in_z]
 
     def begin(self):
         p = self.place
@@ -179,10 +207,39 @@
         self.out[...] = total
 
 
+class ScatterAcross(Scatter):
+    def sizes(self):
+        return [self.half, self.in_xy, None, self.in_z]
+
+    def middle(self):
+        self.pair()
+        for k, dev in enumerate(self.place.along_z):
+            self.go(self.out_xy.at[k + 1], self.in_xy.at[k], 1, dev)
+
+    def end(self):
+        p = self.place
+        self.arrived(1)
+        total = self.grads[0, :, :, p.c].astype(f32) + self.half[0].astype(f32)
+        for k in range(3):
+            total += self.in_xy[k].astype(f32)
+        self.out_xy[0] = total.astype(bf16)
+        for k, (y, x) in enumerate([(p.y, 1 - p.x), (1 - p.y, p.x), (1 - p.y, 1 - p.x)]):
+            self.go(self.out_xy.at[0, y, x], self.in_z.at[k], 3, p.along_xy[k])
+
+    def done(self):
+        p = self.place
+        total = self.ours(0)
+        for k in range(3):
+            total += self.in_xy[k, p.y, p.x].astype(f32)
+        self.arrived(3)
+        for k in range(3):
+            total += self.in_z[k].astype(f32)
+        self.out[...] = total
+
+
 class Direct(Scatter):
-    def __init__(self, *args):
-        super().__init__(*args)
-        self.size_of = [self.half, self.in_xy]
+    def sizes(self):
+        return [self.half, self.in_xy]
 
     def middle(self):
         p = self.place
@@ -244,9 +301,10 @@
     tok, cot, a_in, a_out, m_in, m_out, vecs = take(7)
     reds, (act_out, dx_out) = take(3), take(2)
     wires, grads, halves, outxys, inxys, outzs, inzs = [take(3) for _ in range(7)]
-    (in_direct,) = take(1)
+    in_direct, in_across = take(2)
     tok_near, cot_near, act_near, act_in, dx_near, dx_in = take(6)
     w_in_s, w_one_s, w_out_s, w_two_s, two_s, g_two_s = take(6)
+    pick_s, x_s, dx_s, ds_s = take(4)
     vec_n, vec_g, b_one_s, line_n, line_g = take(5)
     hat1_s, h1_s, qkv_s, p_s, o_s, hat2_s, h2_s, slope_s, a_s, inv_s = take(10)
     dqkv_s, do_s, pack_a, pack_b, pack_c, flat_ai, flat_ao, flat_mi, flat_mo, vec_s = take(10)
@@ -312,18 +370,21 @@
                 pack_c[8 + i:9 + i, 128 + 64 * g:192 + 64 * g] = flat_mo[row, r * d + 128:(r + 1) * d]
         wire_c[(l,) + here] = pack_c[...].astype(bf16)
 
+    across = [(1, 2)]
     gathers = [
         [
-            Gather(place, wires[k].at[l], inxys[k].at[l], gsend.at[l, k], grecv.at[l, k])
+            (GatherAcross if (l, k) in across else Gather)(
+                place, wires[k].at[l], inxys[k].at[l], gsend.at[l, k], grecv.at[l, k]
+            )
             for k in range(3)
         ]
         for l in range(layers)
     ]
     scatters = [
         [
-            (Direct if k == 0 and l == 0 else Scatter)(
+            (Direct if k == 0 and l == 0 else ScatterAcross if (l, k) in across else Scatter)(
                 place, grads[k].at[l], halves[k].at[l], outxys[k].at[l],
-                in_direct if k == 0 and l == 0 else inxys[k].at[l],
+                in_direct if k == 0 and l == 0 else in_across if (l, k) in across else inxys[k].at[l],
                 outzs[k].at[l], inzs[k].at[l], ssend.at[l, k], srecv.at[l, k], reds[k].at[l],
             )
             for k in range(3)
@@ -405,10 +466,21 @@
     gb0.middle()
     gc0.middle()
     ga0.core()
+    gc1.middle()
     ga1.middle()
+    gb1.middle()
     for copy in tok_halo:
         copy.wait_recv()
     x += mm_nt(pick[:, slots:], mm_tn(spread, tok_near[...]).astype(bf16))
+    dx = mm_nt(pick[:, :slots], mm_tn(spread, cot[...]).astype(bf16))
+    pick_s[...] = pick
+    dx_s[...] = dx
+
+    def add_near():
+        for copy in cot_halo:
+            copy.wait_recv()
+        dx_s[...] += mm_nt(pick_s[:, slots:], mm_tn(spread, cot_near[...]).astype(bf16))
+
 
     def tiles_of(wire, l):
         v = wire[l]
@@ -452,7 +524,7 @@
         w_two_s[l] = mm(two_s[:, :d], spread).astype(bf16)
 
     beats = [
-        [lambda: gb1.middle(), lambda: gc1.middle(), lambda: gb0.core(), lambda: gc0.core(), lambda: ga1.core()],
+        [lambda: None, lambda: None, lambda: (gb0.core(), add_near()), lambda: gc0.core(), lambda: ga1.core()],
         [lambda: gb1.core(), lambda: gc1.core(), lambda: None, lambda: None, lambda: None],
     ]
     for l in range(layers):
@@ -467,18 +539,22 @@
         qkv_s[l, :, d:2 * d] = projected[:, d:2 * d].astype(bf16)
         qkv_s[l, :, 2 * d:] = (projected[:, 2 * d:] + vec_n[l, 3:4]).astype(bf16)
         beats[l][0]()
-        for i in range(IMAGES_HERE):
-            at = slice(i * ROWS, (i + 1) * ROWS)
-            for head in range(heads):
-                q = qkv_s[l, at, head * HD:(head + 1) * HD]
-                key = qkv_s[l, at, d + head * HD:d + (head + 1) * HD]
-                val = qkv_s[l, at, 2 * d + head * HD:2 * d + (head + 1) * HD]
-                scores = jnp.where(valid_keys[i], mm_nt(q, key), masked_fill)
-                e = jnp.exp(scores - jnp.max(scores, axis=-1, keepdims=True))
-                p = e * (1.0 / jnp.sum(e, axis=-1, keepdims=True))
-                p_s[l, i, head] = p
-                o_s[l, at, head * HD:(head + 1) * HD] = mm(p.astype(bf16), val).astype(bf16)
-            beats[l][1 + i]()
+        parts = [(i, head) for i in range(IMAGES_HERE) for head in range(heads)]
+        at_of = lambda i: slice(i * ROWS, (i + 1) * ROWS)
+        lanes = lambda group, head: slice(group * d + head * HD, group * d + (head + 1) * HD)
+        for i, head in parts:
+            scores = mm_nt(qkv_s[l, at_of(i), lanes(0, head)], qkv_s[l, at_of(i), lanes(1, head)])
+            scores = jnp.where(valid_keys[i], scores, masked_fill)
+            e = jnp.exp(scores - jnp.max(scores, axis=-1, keepdims=True))
+            p = e * (1.0 / jnp.sum(e, axis=-1, keepdims=True))
+            p_s[l, i, head] = p
+            ds_s[i, head] = p.astype(bf16)
+        beats[l][1]()
+        for i, head in parts:
+            o_s[l, at_of(i), lanes(0, head)] = mm(
+                ds_s[i, head], qkv_s[l, at_of(i), lanes(2, head)]
+            ).astype(bf16)
+        beats[l][2]()
         gb.done()
         beats[l][3]()
         unpack_b(l)
@@ -494,16 +570,8 @@
         unpack_c(l)
         x = x1 + (mm(a_s[l], w_two_s[l]) + vec_g[l, 7:8])
 
-    x_low = mm_nt(x.astype(bf16), spread).astype(bf16)
-    act_near[...] = mm_tn(x_low, pick[:, slots:]).astype(bf16)
-    for copy in act_halo:
-        copy.start()
-    act_own = mm_tn(x_low, pick[:, :slots]).astype(bf16)
-
-    for copy in cot_halo:
-        copy.wait_recv()
-    dx = mm_nt(pick[:, :slots], mm_tn(spread, cot[...]).astype(bf16))
-    dx += mm_nt(pick[:, slots:], mm_tn(spread, cot_near[...]).astype(bf16))
+    x_s[...] = x.astype(bf16)
+    dx = dx_s[...]
 
     def cut(w, pieces):
         return [w[:, 128 * k:128 * k + 128].reshape(n, 8, 128) for k in range(pieces)]
@@ -515,7 +583,7 @@
         return v.reshape(4, 2, 2, 2, BLOCK, 128 * half)
 
     beats = [
-        [lambda: (sa1.middle(), sc1.end()), lambda: sc0.middle(),
+        [lambda: sa1.middle(), lambda: (sc0.middle(), sc1.end()),
          lambda: (sb1.end(), sb0.middle()), lambda: None],
         [lambda: None, lambda: sc1.middle(), lambda: sb1.middle(), lambda: None],
     ]
@@ -556,20 +624,25 @@
         beats[l][1]()
         sb.begin()
         do_s[...] = mm_nt(db, w_out_s[l]).astype(bf16)
-        for i in range(IMAGES_HERE):
-            at = slice(i * ROWS, (i + 1) * ROWS)
-            for head in range(heads):
-                q_at = slice(head * HD, (head + 1) * HD)
-                k_at = slice(d + head * HD, d + (head + 1) * HD)
-                v_at = slice(2 * d + head * HD, 2 * d + (head + 1) * HD)
-                do = do_s[at, q_at]
-                p = p_s[l, i, head]
-                dp = mm_nt(do, qkv_s[l, at, v_at])
-                ds = (p * (dp - jnp.sum(p * dp, axis=-1, keepdims=True))).astype(bf16)
-                dqkv_s[at, q_at] = (mm(ds, qkv_s[l, at, k_at]) * (1.0 / math.sqrt(HD))).astype(bf16)
-                dqkv_s[at, k_at] = mm_tn(ds, qkv_s[l, at, q_at]).astype(bf16)
-                dqkv_s[at, v_at] = mm_tn(p.astype(bf16), do).astype(bf16)
-            beats[l][2 + i]()
+        parts = [(i, head) for i in range(IMAGES_HERE) for head in range(heads)]
+        at_of = lambda i: slice(i * ROWS, (i + 1) * ROWS)
+        lanes = lambda group, head: slice(group * d + head * HD, group * d + (head + 1) * HD)
+        for i, head in parts:
+            p = p_s[l, i, head]
+            dp = mm_nt(do_s[at_of(i), lanes(0, head)], qkv_s[l, at_of(i), lanes(2, head)])
+            ds_s[i, head] = (p * (dp - jnp.sum(p * dp, axis=-1, keepdims=True))).astype(bf16)
+        beats[l][2]()
+        for i, head in parts:
+            at = at_of(i)
+            ds = ds_s[i, head]
+            dqkv_s[at, lanes(0, head)] = (
+                mm(ds, qkv_s[l, at, lanes(1, head)]) * (1.0 / math.sqrt(HD))
+            ).astype(bf16)
+            dqkv_s[at, lanes(1, head)] = mm_tn(ds, qkv_s[l, at, lanes(0, head)]).astype(bf16)
+            dqkv_s[at, lanes(2, head)] = mm_tn(
+                p_s[l, i, head].astype(bf16), do_s[at, lanes(0, head)]
+            ).astype(bf16)
+        beats[l][3]()
         dqkv = dqkv_s[:, :640]
         line_n[2:3] = rows_sum(dqkv_s[:, :d].astype(f32))
         line_n[3:4] = rows_sum(dqkv_s[:, 2 * d:3 * d].astype(f32))
@@ -588,27 +661,32 @@
     high = dx.astype(bf16)
     low = (dx - high.astype(f32)).astype(bf16)
     high = mm_nt(high, spread).astype(bf16)
-    dx_near[...] = mm_tn(high, pick[:, slots:]).astype(bf16)
+    dx_near[...] = mm_tn(high, pick_s[:, slots:]).astype(bf16)
     for copy in dx_halo:
         copy.start()
     sa1.end()
     sa0.middle()
+    x_low = mm_nt(x_s[...], spread).astype(bf16)
+    act_near[...] = mm_tn(x_low, pick_s[:, slots:]).astype(bf16)
+    for copy in act_halo:
+        copy.start()
     sc0.end()
     low = mm_nt(low, spread).astype(bf16)
-    dx_own = mm_tn(high, pick[:, :slots]) + mm_tn(low, pick[:, :slots])
+    dx_own = mm_tn(high, pick_s[:, :slots]) + mm_tn(low, pick_s[:, :slots])
+    act_own = mm_tn(x_low, pick_s[:, :slots]).astype(bf16)
+    sb0.end()
     sc1.done()
-    sb0.end()
     sb1.done()
+    for copy in dx_halo:
+        copy.wait_recv()
+    dx_out[...] = dx_own + dx_in[...].astype(f32)
     for copy in act_halo:
         copy.wait_recv()
     act_out[...] = act_own + act_in[...]
-    for copy in dx_halo:
-        copy.wait_recv()
-    dx_out[...] = dx_own + dx_in[...].astype(f32)
     sa1.done()
     sc0.done()
+    sa0.done()
     sb0.done()
-    sa0.done()
     for copy in tok_halo + cot_halo + act_halo + dx_halo:
         copy.wait_send()
     for group in gathers + scatters:
@@ -629,7 +707,7 @@
         boxes((4, 2, 2, 2), bf16) + boxes((4, 2, 2, 2), bf16)
         + boxes((4, 2, 2), bf16) + boxes((4, 2, 2), bf16) + boxes((3, 4), bf16)
         + boxes((3,), bf16) + boxes((3,), bf16)
-        + [pltpu.VMEM((15,) + shapes[0], bf16)]
+        + [pltpu.VMEM((15,) + shapes[0], bf16), pltpu.VMEM((3, 2, 2) + shapes[2], bf16)]
         + [pltpu.VMEM((d, slots), bf16)] * 6
         + [
             pltpu.VMEM((layers, wide, 640), bf16),
@@ -638,6 +716,10 @@
             pltpu.VMEM((layers, hidden_units, wide), bf16),
             pltpu.VMEM((hidden_units, 256), bf16),
             pltpu.VMEM((hidden_units, d), f32),
+            pltpu.VMEM((rows, 2 * slots), bf16),
+            pltpu.VMEM((rows, wide), bf16),
+            pltpu.VMEM((rows, wide), f32),
+            pltpu.VMEM((IMAGES_HERE, d // HD, ROWS, ROWS), bf16),
             pltpu.VMEM((layers, BLOCK, d), f32),
             pltpu.VMEM((layers, BLOCK, wide), f32),
             pltpu.VMEM((layers, 8, hidden_units), f32),

time: 54 us -> 51.1 us (0.946)
  Pallas kernels: 53.1 us -> 50.3 us
    pallas_call x1, Pallas kernels: 51.3 us -> 48.4 us  [fused(): pl.pallas_call(functools.partial(fused_kernel, n, layers, d), out_shape=t...]
where the time goes in v4:
time: 51.1 us; the launch traced here: 51 us
  Pallas kernels  50.3 us (98%)
  between operations  0.64 us (1%)
    pallas_call x1, Pallas kernels, fused(): pl.pallas_call(functools.partial(fused_kernel, n, layers, d), out_shape=t...  48.4 us
    pallas_call x1, Pallas kernels, local_fused(): pl.pallas_call(functools.partial(flatten_kernel, n, layers, d), out_shape...  1.88 us

profile of v4, /device:TPU:0, one launch (start us, length us, event | category | flops | bytes accessed | tf_op | source)
XLA Modules:
  0.0 51.0 jit_solution(4405806174322912617)
XLA Ops:
  0.6 48.4 %two_layers.1 = (f32[2,16,256]{2,1,0:T(8,128)}, f32[2,16,384]{2,1,0:T(8,128)}, f32[2,16,256]{2,1,0:T(8,128)}, bf16[192,256]{1,0:T(8,128)(2,1)}, f32[192,256]{1,0:T(8,128)}) custom-call(s32[2,32]{1,0:T(2,128)} %bitcast.7, bf16[192,256]{1,0:T(8,128)(2,1)} %bitcast.5, bf16[192,256]{1,0:T(8,128)(2,1)} %bitcast.6, bf16[2,3456]{1,0:T(2,128)(2,1)} %refs_2_.1, ...), custom_call_target="tpu_custom_call" | custom-call | tf_op jit(solution)/shard_map/two_layers/pallas_call | solution.py:747
  49.1 1.9 %flatten.1 = (bf16[192,256]{1,0:T(8,128)(2,1)}, f32[192,256]{1,0:T(8,128)}, f32[2,3456]{1,0:T(2,128)}, f32[2,1152]{1,0:T(2,128)}, f32[2,4608]{1,0:T(2,128)}, /*index=5*/f32[2,4608]{1,0:T(2,128)}, f32[2,72]{1,0:T(2,128)}) custom-call(f32[2,16,256]{2,1,0:T(8,128)} %get-tuple-element.19.red_a, f32[2,16,384]{2,1,0:T(8,128)} %get-tuple-element.20.red_b, ...), custom_call_target="tpu_custom_call" | custom-call | tf_op jit(solution)/shard_map/flatten/pallas_call | solution.py:805

commit v5 on v4

--- a/solution.py
+++ b/solution.py
@@ -611,6 +611,7 @@
         for k in range(4):
             line_n[8 + k:9 + k] = g_b1[:, k * d:(k + 1) * d]
         dh2 = mm_nt(du, w_one_s[l])
+        g_one = mm_tn(h2_s[l], du)
         dv, g_g2, g_c2 = norm_padded_back(dh2, hat2_s[l], inv_s[l, 1], vec_g[l, 5:6], d)
         line_g[5:6], line_g[6:7] = g_g2, g_c2
         dx1 = dx + dv
@@ -619,7 +620,7 @@
         g_out = mm_tn(o_s[l], mm_nt(db, spread).astype(bf16))
         g_out = jnp.concatenate([g_out, jnp.zeros((d, 256 - d), f32)], axis=1).astype(bf16)
         t6, t7 = cut(mm_tn(spread, g_out), 2)
-        t0, t1, t2, t3, t4, t5 = cut(mm_tn(h2_s[l], du), 6)
+        t0, t1, t2, t3, t4, t5 = cut(g_one, 6)
         grads[1][l] = block(fold((t0, t1, t2), t3, sub) + fold((t4, t5, t6), t7, sub))
         beats[l][1]()
         sb.begin()
@@ -647,12 +648,13 @@
         line_n[2:3] = rows_sum(dqkv_s[:, :d].astype(f32))
         line_n[3:4] = rows_sum(dqkv_s[:, 2 * d:3 * d].astype(f32))
         dh = mm_nt(dqkv, w_in_s[l])
+        g_in = mm_tn(h1_s[l], dqkv)
         dv, g_g1, g_c1 = norm_padded_back(dh, hat1_s[l], inv_s[l, 0], vec_g[l, 0:1], d)
         line_g[0:1], line_g[1:2] = g_g1, g_c1
         lines = (line_n[...] + mm_nt(line_g[...].astype(bf16), spread)).astype(bf16)
         vec_rows = sum(mm_tn(windows[k], lines[:, 64 * k:64 * k + 64]) for k in range(3))
         vec_rows = jnp.concatenate([vec_rows, jnp.zeros((wide, 64), f32)], axis=1).reshape(n, 8, 128)
-        t0, t1, t2, t3, t4 = cut(mm_tn(h1_s[l], dqkv), 5)
+        t0, t1, t2, t3, t4 = cut(g_in, 5)
         t4 = jnp.where(low_lanes, t4 + vec_rows, tail)
         grads[0][l] = block(fold((t0, t1, t2), t3, sub) + [t4])
         sa.begin()
@@ -913,6 +915,7 @@
         g_one = mm_tn(h2_s[l], du).astype(bf16)
         grad_s[l, :d, 4 * d:8 * d] = mm_nt(g_one, perm[...]).astype(bf16)
         dh2 = mm_nt(du, w_one_s[l])
+        g_one = mm_tn(h2_s[l], du)
         dv, g_g2, g_c2 = norm_backward(dh2, hat2_s[l], inv_s[l, 1], v_of(l, 5))
         dx1 = dx + dv
         db = dx1.astype(bf16)

time: 51.1 us -> 50.3 us (0.984)
  Pallas kernels: 50.3 us -> 49.5 us
    pallas_call x1, Pallas kernels: 48.4 us -> 47.6 us  [fused(): pl.pallas_call(functools.partial(fused_kernel, n, layers, d), out_shape=t...]
where the time goes in v5:
time: 50.3 us; the launch traced here: 50.1 us
  Pallas kernels  49.5 us (98%)
  between operations  0.64 us (1%)
    pallas_call x1, Pallas kernels, fused(): pl.pallas_call(functools.partial(fused_kernel, n, layers, d), out_shape=t...  47.6 us
    pallas_call x1, Pallas kernels, local_fused(): pl.pallas_call(functools.partial(flatten_kernel, n, layers, d), out_shape...  1.88 us

profile of v5, /device:TPU:0, one launch (start us, length us, event | category | flops | bytes accessed | tf_op | source)
XLA Modules:
  0.0 50.1 jit_solution(8234658773721100410)
XLA Ops:
  0.6 47.6 %two_layers.1 = (f32[2,16,256]{2,1,0:T(8,128)}, f32[2,16,384]{2,1,0:T(8,128)}, f32[2,16,256]{2,1,0:T(8,128)}, bf16[192,256]{1,0:T(8,128)(2,1)}, f32[192,256]{1,0:T(8,128)}) custom-call(s32[2,32]{1,0:T(2,128)} %bitcast.7, bf16[192,256]{1,0:T(8,128)(2,1)} %bitcast.5, bf16[192,256]{1,0:T(8,128)(2,1)} %bitcast.6, bf16[2,3456]{1,0:T(2,128)(2,1)} %refs_2_.1, ...), custom_call_target="tpu_custom_call" | custom-call | tf_op jit(solution)/shard_map/two_layers/pallas_call | solution.py:749
  48.2 1.9 %flatten.1 = (bf16[192,256]{1,0:T(8,128)(2,1)}, f32[192,256]{1,0:T(8,128)}, f32[2,3456]{1,0:T(2,128)}, f32[2,1152]{1,0:T(2,128)}, f32[2,4608]{1,0:T(2,128)}, /*index=5*/f32[2,4608]{1,0:T(2,128)}, f32[2,72]{1,0:T(2,128)}) custom-call(f32[2,16,256]{2,1,0:T(8,128)} %get-tuple-element.19.red_a, f32[2,16,384]{2,1,0:T(8,128)} %get-tuple-element.20.red_b, ...), custom_call_target="tpu_custom_call" | custom-call | tf_op jit(solution)/shard_map/flatten/pallas_call | solution.py:807
